TPU v7x, 256 devices: a whole 4x4x8 slice. The times are simulated.
256 devices in a mesh: tok: 64 (over y, x, z_hi, core), hid: 4 (over z_lo).
Axes of the slice: x: 4, y: 4, z: 8 (z_hi: 2, z_lo: 4; z = z_hi * 4 + z_lo), core: 2. Of those that a mesh axis runs over, the one named last changes fastest.
Arguments:
- block_input: bfloat16 [512, 128, 1024], P('hid', 'tok'), may hold values from -6 to 6
- out_grad: bfloat16 [512, 128, 1024], P('hid', 'tok'), may hold values from -6 to 6
- norm_gain: float32 [128, 1024], P('tok'), may hold values from 0.25 to 1.75
- w_in: bfloat16 [128, 1024, 2048], P('tok', None, 'hid'), may hold values from -0.1875 to 0.1875
- w_out: bfloat16 [128, 2048, 1024], P('tok', 'hid'), may hold values from -0.125 to 0.125
Outputs:
- input_grad: bfloat16 [512, 128, 1024], P('hid', 'tok')
- grad_in: bfloat16 [128, 1024, 2048], P('tok', None, 'hid')
- grad_out: bfloat16 [128, 2048, 1024], P('tok', 'hid')
All inputs are finite; a program needn't handle non-finite values.
Results may differ from a plain program's by a relative error of at most 0.0061.
Values may be sent and summed in bfloat16 or wider, within the bound.
A program may use at most 64 MiB of HBM per device.

v0:
```python
import jax
import jax.numpy as jnp
from jax import lax
from jax.sharding import PartitionSpec as P

TOKENS = 128
WIDTH = 1024
HEAD = 8


EPS = 1e-06


def gelu_tanh(value):
    return 0.5 * value * (1.0 + jnp.tanh(0.7978845608 * (value + 0.044715 * value * value * value)))


def head_major(array):
    samples, local_tok, width = array.shape
    return array.reshape(samples, local_tok, TOKENS, HEAD).transpose(2, 1, 3, 0)


def normalize(mixed, gain_col):
    mixed_f = mixed.astype(jnp.float32)
    scale = lax.rsqrt(jnp.mean(mixed_f * mixed_f, axis=1, keepdims=True) + EPS)
    return (scale, (mixed_f * scale * gain_col).astype(jnp.bfloat16))


def per_device(block_input, out_grad, norm_gain, w_in, w_out):
    own_rows, local_tok, width = block_input.shape
    gain_col = norm_gain[:, :, None]
    all_in, all_grad = (
        lax.all_gather(block_input, "hid", axis=0, tiled=True),
        lax.all_gather(out_grad, "hid", axis=0, tiled=True),
    )
    mixed_all, dmix_all = (
        lax.all_to_all(head_major(all_in), "tok", split_axis=0, concat_axis=1, tiled=True),
        lax.all_to_all(head_major(all_grad), "tok", split_axis=0, concat_axis=1, tiled=True),
    )
    mixed_all = mixed_all.reshape(local_tok, width, -1)
    dmix_all = dmix_all.reshape(local_tok, width, -1)
    scale_all, normed_all = normalize(mixed_all, gain_col)
    start = lax.axis_index("hid") * own_rows
    mixed_own = lax.dynamic_slice_in_dim(mixed_all, start, own_rows, 2)
    scale_own = lax.dynamic_slice_in_dim(scale_all, start, own_rows, 2)
    pre = jnp.einsum("tdb,tdf->tbf", normed_all, w_in, preferred_element_type=jnp.float32)
    act, pull = jax.vjp(gelu_tanh, pre)
    act_b = act.astype(jnp.bfloat16)
    act_grad = jnp.einsum("tdb,tfd->tbf", dmix_all, w_out, preferred_element_type=jnp.float32)
    pre_grad = pull(act_grad)[0].astype(jnp.bfloat16)
    grad_out = jnp.einsum(
        "tbf,tdb->tfd", act_b, dmix_all, preferred_element_type=jnp.float32
    ).astype(jnp.bfloat16)
    grad_in = jnp.einsum(
        "tdb,tbf->tdf", normed_all, pre_grad, preferred_element_type=jnp.float32
    ).astype(jnp.bfloat16)
    partial_grad = jnp.einsum("tbf,tdf->tdb", pre_grad, w_in, preferred_element_type=jnp.float32)
    normed_grad = lax.psum_scatter(partial_grad, "hid", scatter_dimension=2, tiled=True)
    mixed_f = mixed_own.astype(jnp.float32)
    upper = normed_grad * gain_col
    inner = jnp.sum(upper * mixed_f, axis=1, keepdims=True)
    mixed_back = (
        scale_own * upper - mixed_f * scale_own * scale_own * scale_own * inner / WIDTH
    ).astype(jnp.bfloat16)
    returned = lax.all_to_all(
        mixed_back.reshape(local_tok, TOKENS, HEAD, own_rows),
        "tok",
        split_axis=1,
        concat_axis=0,
        tiled=True,
    )
    returned = returned.transpose(3, 1, 0, 2).reshape(own_rows, local_tok, width)
    input_grad = (out_grad.astype(jnp.float32) + returned.astype(jnp.float32)).astype(jnp.bfloat16)
    return (input_grad, grad_in, grad_out)


def solution(mesh):
    in_specs = (
        P("hid", "tok", None),
        P("hid", "tok", None),
        P("tok", None),
        P("tok", None, "hid"),
        P("tok", "hid", None),
    )
    out_specs = (P("hid", "tok", None), P("tok", None, "hid"), P("tok", "hid", None))
    return jax.shard_map(
        per_device, mesh=mesh, in_specs=in_specs, out_specs=out_specs, check_vma=False
    )
```

profile of v0, /device:TPU:1, one launch (start us, length us, event | category | flops | bytes accessed | tf_op | source)
XLA Modules:
  0.0 361.3 jit_solution(12264730030906963151)
XLA Ops:
  7.2 2.2 copy.27
  9.4 56.9 %all-gather.3.cloned.1.call-done = bf16[512,2,1024]{0,2,1:T(8,128)(2,1)} async-done(((bf16[128,2,1024]{0,2,1:T(8,128)(2,1)}), bf16[512,2,1024]{0,2,1:T(8,128)(2,1)}) %all-gather.3.cloned.1.call-update) | async-done | bytes 2097168 | tf_op jit(solution)/shard_map/all_gather | solution.py:33
  66.3 3.2 copy.28
  69.5 9.7 %all-to-all-start = ((bf16[128,2,8,512]{3,2,1,0:T(8,128)(2,1)}), bf16[128,2,8,512]{3,2,1,0:T(8,128)(2,1)}, u32[]{:S(2)}, u32[]{:S(2)}) async-start(bf16[128,2,8,512]{3,2,1,0:T(8,128)(2,1)} %copy.28), calls=%async_computation | async-start | bytes 4194304 | tf_op jit(solution)/shard_map/all_to_all | solution.py:37
  79.2 0.0 all-gather.5.cloned.1.call-start
  79.3 1.2 copy.26
  80.5 79.7 %all-gather.5.cloned.1.call-done = bf16[512,2,1024]{0,2,1:T(8,128)(2,1)} async-done(((bf16[128,2,1024]{0,2,1:T(8,128)(2,1)}), bf16[512,2,1024]{0,2,1:T(8,128)(2,1)}) %all-gather.5.cloned.1.call-update) | async-done | bytes 2097168 | tf_op jit(solution)/shard_map/all_gather | solution.py:34
  160.1 3.2 copy.32
  163.4 12.3 %all-to-all-start.1 = ((bf16[128,2,8,512]{3,2,1,0:T(8,128)(2,1)}), bf16[128,2,8,512]{3,2,1,0:T(8,128)(2,1)}, u32[]{:S(2)}, u32[]{:S(2)}) async-start(bf16[128,2,8,512]{3,2,1,0:T(8,128)(2,1)} %copy.32), calls=%async_computation.1 | async-start | bytes 4194304 | tf_op jit(solution)/shard_map/all_to_all | solution.py:38
  175.7 3.1 copy.29
  178.8 2.1 multiply_reduce_fusion
  180.9 48.6 %all-to-all-done.1 = bf16[128,2,8,512]{3,2,1,0:T(8,128)(2,1)} async-done(((bf16[128,2,8,512]{3,2,1,0:T(8,128)(2,1)}), bf16[128,2,8,512]{3,2,1,0:T(8,128)(2,1)}, u32[]{:S(2)}, u32[]{:S(2)}) %all-to-all-start.1) | async-done | bytes 2097184 | tf_op jit(solution)/shard_map/all_to_all | solution.py:38
  229.5 1.9 copy.33
  231.5 0.2 copy-done.7
  231.7 1.6 fusion.25
  233.3 0.5 copy-done.2
  233.8 4.1 %fusion.4 = (bf16[2,512,512]{2,1,0:T(8,128)(2,1)S(1)}, f32[2,512,512]{2,1,0:T(8,128)}) fusion(f32[2,512,512]{2,1,0:T(8,128)S(1)} %fusion.25, bf16[2,1024,512]{2,1,0:T(8,128)(2,1)S(1)} %copy-done, bf16[2,1024,512]{2,1,0:T(8,128)(2,1)S(1)} %bitcast.38, f32[2,1024]{1,0:T(2,128)S(1)} %copy-done.8, f32[2,512]{1,0:T(2,128)S(1)} %add_rsqrt_fusion), kind=kOutput, calls=%fused_computation.11 | convolution fusion | flops 1090519040 | bytes 9449472 | tf_op jit(solution)/shard_map/tdb,tdf->tbf/dot_general | solution.py:46
  237.9 1.0 copy-done.5
  238.9 3.2 convolution_bitcast_fusion
  242.2 1.1 constant_dynamic-slice_fusion
  243.3 0.2 copy.44
  243.5 74.3 %reduce-scatter.2.cloned.1.call-done = f32[2,1024,128]{1,2,0:T(8,128)} async-done(((f32[2,1024,512]{1,2,0:T(8,128)}), f32[2,1024,128]{1,2,0:T(8,128)}) %reduce-scatter.2.cloned.1.call-update) | async-done | bytes 1048592 | tf_op jit(solution)/shard_map/reduce_scatter | solution.py:58
  317.8 2.8 fusion.11
  320.6 1.3 copy.36
  322.0 0.9 copy.37
  322.8 12.4 %all-to-all-start.2 = ((bf16[2,128,8,128]{3,2,0,1:T(8,128)(2,1)}), bf16[2,128,8,128]{3,2,0,1:T(8,128)(2,1)S(1)}, u32[]{:S(2)}, u32[]{:S(2)}) async-start(bf16[2,128,8,128]{3,2,0,1:T(8,128)(2,1)} %copy.37), calls=%async_computation.3 | async-start | bytes 1048576 | tf_op jit(solution)/shard_map/all_to_all | solution.py:65
  335.3 4.6 %convolution_convert_fusion.1 = bf16[2,1024,512]{2,1,0:T(8,128)(2,1)} fusion(bf16[2,512,512]{2,1,0:T(8,128)(2,1)} %copy-done.5, bf16[2,1024,512]{2,1,0:T(8,128)(2,1)} %bitcast.37, f32[2,1024]{1,0:T(2,128)S(1)} %copy-done.8, f32[2,512]{1,0:T(2,128)S(1)} %add_rsqrt_fusion), kind=kOutput, calls=%fused_computation.16 | convolution fusion | flops 1078984704 | bytes 5255168 | tf_op jit(solution)/shard_map/tdb,tbf->tdf/dot_general | solution.py:54
  340.0 3.1 convolution_convert_fusion
  343.1 10.3 %all-to-all-done.2 = bf16[2,128,8,128]{3,2,0,1:T(8,128)(2,1)S(1)} async-done(((bf16[2,128,8,128]{3,2,0,1:T(8,128)(2,1)}), bf16[2,128,8,128]{3,2,0,1:T(8,128)(2,1)S(1)}, u32[]{:S(2)}, u32[]{:S(2)}) %all-to-all-start.2) | async-done | bytes 524320 | tf_op jit(solution)/shard_map/all_to_all | solution.py:65
  353.4 0.1 copy.38
  353.5 0.1 fusion.14
  353.6 1.1 copy.40
  (25 shorter events, 0.2 us)
Async XLA Ops:
  7.2 226.2 %copy-start = (bf16[2,1024,512]{2,1,0:T(8,128)(2,1)S(1)}, bf16[2,1024,512]{2,1,0:T(8,128)(2,1)}, u32[]{:S(2)}) copy-start(bf16[2,1024,512]{2,1,0:T(8,128)(2,1)} %param.8) | copy-start | bytes 6291460
  7.2 59.1 %all-gather.3.cloned.1.call-start = ((), (), s32[]{:S(2)}) async-start(), calls=%async_computation.4 | async-start | bytes 2621440 | tf_op jit(solution)/shard_map/all_gather | solution.py:33
  69.5 9.7 %copy-start.6 = (bf16[128,2,1024]{2,1,0:T(2,128)(2,1)S(1)}, bf16[128,2,1024]{2,1,0:T(2,128)(2,1)}, u32[]{:S(2)}) copy-start(bf16[128,2,1024]{2,1,0:T(2,128)(2,1)} %param.6) | copy-start | bytes 1572868
  69.5 93.8 %all-to-all-start = ((bf16[128,2,8,512]{3,2,1,0:T(8,128)(2,1)}), bf16[128,2,8,512]{3,2,1,0:T(8,128)(2,1)}, u32[]{:S(2)}, u32[]{:S(2)}) async-start(bf16[128,2,8,512]{3,2,1,0:T(8,128)(2,1)} %copy.28), calls=%async_computation | async-start | bytes 4194304 | tf_op jit(solution)/shard_map/all_to_all | solution.py:37
  79.2 80.9 %all-gather.5.cloned.1.call-start = ((), (), s32[]{:S(2)}) async-start(), calls=%async_computation.5 | async-start | bytes 2621440 | tf_op jit(solution)/shard_map/all_gather | solution.py:34
  163.4 66.1 %all-to-all-start.1 = ((bf16[128,2,8,512]{3,2,1,0:T(8,128)(2,1)}), bf16[128,2,8,512]{3,2,1,0:T(8,128)(2,1)}, u32[]{:S(2)}, u32[]{:S(2)}) async-start(bf16[128,2,8,512]{3,2,1,0:T(8,128)(2,1)} %copy.32), calls=%async_computation.1 | async-start | bytes 4194304 | tf_op jit(solution)/shard_map/all_to_all | solution.py:38
  175.7 142.1 %reduce-scatter.2.cloned.1.call-start = ((), (), s32[]{:S(2)}) async-start(), calls=%async_computation.6 | async-start | bytes 5242880 | tf_op jit(solution)/shard_map/reduce_scatter | solution.py:58
  229.5 2.2 copy-start.7
  231.5 1.9 copy-start.3
  231.7 2.1 copy-start.2
  231.7 2.1 copy-start.8
  237.9 1.1 copy-start.5
  322.8 30.6 %all-to-all-start.2 = ((bf16[2,128,8,128]{3,2,0,1:T(8,128)(2,1)}), bf16[2,128,8,128]{3,2,0,1:T(8,128)(2,1)S(1)}, u32[]{:S(2)}, u32[]{:S(2)}) async-start(bf16[2,128,8,128]{3,2,0,1:T(8,128)(2,1)} %copy.37), calls=%async_computation.3 | async-start | bytes 1048576 | tf_op jit(solution)/shard_map/all_to_all | solution.py:65
  335.3 4.7 %copy-start.4 = (bf16[2,64,2,8,512]{4,3,2,1,0:T(8,128)(2,1)S(1)}, bf16[2,64,2,8,512]{4,3,2,1,0:T(8,128)(2,1)}, u32[]{:S(2)}) copy-start(bf16[2,64,2,8,512]{4,3,2,1,0:T(8,128)(2,1)} %copy-done.3) | copy-start | bytes 6291460
  335.3 4.6 %copy-start.9 = (f32[2,512,512]{2,1,0:T(8,128)S(1)}, f32[2,512,512]{2,1,0:T(8,128)}, u32[]{:S(2)}) copy-start(f32[2,512,512]{2,1,0:T(8,128)} %get-tuple-element.10) | copy-start | bytes 6291460
  340.0 13.5 %copy-start.1 = (bf16[128,2,1024]{0,2,1:T(8,128)(2,1)S(1)}, bf16[128,2,1024]{0,2,1:T(8,128)(2,1)}, u32[]{:S(2)}) copy-start(bf16[128,2,1024]{0,2,1:T(8,128)(2,1)} %copy.26) | copy-start | bytes 1572868
Sparse Core Ops, SparseCore 0:
  10.4 55.8 all-gather.2
  82.4 77.6 all-gather.4
  242.3 75.4 reduce-scatter.1
where the time goes:
time: 363 us; the launch traced here: 361 us
  waiting for transfers between devices  270 us (74%)
  starting transfers between devices  34.5 us (10%)
  local copies, waits for them, and re-layouts  21.3 us (6%)
  matrix products  16.7 us (5%)
  between operations  13.9 us (4%)
  other arithmetic  5.02 us (1%)
    all_gather x1, waiting for transfers between devices, per_device(): lax.all_gather(out_grad, 'hid', axis=0, tiled=True)  79.7 us
    reduce_scatter x1, waiting for transfers between devices, per_device(): lax.psum_scatter(partial_grad, 'hid', scatter_dimension=2, tiled=True)  74.3 us
    all_gather x1, waiting for transfers between devices, per_device(): lax.all_gather(block_input, 'hid', axis=0, tiled=True)  56.9 us
    all_to_all x1, waiting for transfers between devices, per_device(): lax.all_to_all(head_major(all_grad), 'tok', split_axis=0, concat_axis=1,...  48.6 us
    all_to_all x1, starting transfers between devices, per_device(): lax.all_to_all(mixed_back.reshape(local_tok, TOKENS, HEAD, own_rows), 'to...  12.4 us
    all_to_all x1, starting transfers between devices, per_device(): lax.all_to_all(head_major(all_grad), 'tok', split_axis=0, concat_axis=1,...  12.3 us
    all_to_all x1, waiting for transfers between devices, per_device(): lax.all_to_all(mixed_back.reshape(local_tok, TOKENS, HEAD, own_rows), 'to...  10.3 us
    all_to_all x1, starting transfers between devices, per_device(): lax.all_to_all(head_major(all_in), 'tok', split_axis=0, concat_axis=1, ti...  9.68 us
  transfers between devices with their start and end apart: 6, of which 5 were waited for; matrix products, arithmetic and copies ran while one was open for 5% of the time, Pallas kernels for 0%

commit v1 on v0

v1 whole, which is shorter than its diff:
```python
import functools

import jax
import jax.numpy as jnp
from jax import lax
from jax.experimental import pallas as pl
from jax.experimental.pallas import tpu as pltpu
from jax.sharding import PartitionSpec as P

TOKENS = 128
WIDTH = 1024
HEAD = 8
EPS = 1e-06
MESH = pl.DeviceIdType.MESH

COLUMNS = 16
PEERS = 32
PLANES = 8
OUT, PASS = 8, 9

LEFT = {
    0: [(OUT, "c0x"), (PASS, "c1x")],
    1: [(OUT, PASS), ("s1", "s1"), ("s2", "s2"), ("s3", "s3"), ("c0", "c0"), ("c1", "c1")],
    2: [("s2", "s2"), ("s3", "s3"), ("c0", "c0"), ("c1", "c1")],
    3: [("s3", "s3"), ("c0", "c0"), ("c1", "c1")],
}


def mirrored(slot):
    if not isinstance(slot, str):
        return slot
    return slot[0] + str(3 - int(slot[1])) + slot[2:]


RIGHT = {3 - zl: [(mirrored(a), mirrored(b)) for a, b in items] for zl, items in LEFT.items()}

BACK_RIGHT = {
    0: ["c1", "c0", "s3", "s2", "p1", "s1"],
    1: ["c1", "c0", "s3", "s2"],
    2: ["c1", "c0", "s3"],
    3: ["c1", "c0"],
}
BACK_LEFT = {3 - zl: [mirrored(a) for a in items] for zl, items in BACK_RIGHT.items()}


def place():
    tok, zl = lax.axis_index("tok"), lax.axis_index("hid")
    core, half, column = lax.rem(tok, 2), lax.rem(tok // 2, 2), tok // 4
    return column, half, core, zl


def device(column, half, core, zl):
    return (column * 4 + half * 2 + core, zl)


def z_neighbour(column, half, core, zl, step):
    z = lax.rem(half * 4 + zl + PLANES + step, PLANES)
    return device(column, z // 4, core, lax.rem(z, 4))


def plane_peer(column, half, core, zl, ahead):
    peer = lax.rem(column * 2 + core + ahead, PEERS)
    return peer, device(peer // 2, half, lax.rem(peer, 2), zl)


def wait_for(ref, sem):
    pltpu.make_async_copy(ref, ref, sem).wait()


def greet(here):
    barrier = pltpu.get_barrier_semaphore()

    def signal(ahead, carry):
        _, target = plane_peer(*here, ahead)
        pl.semaphore_signal(barrier, inc=1, device_id=target, device_id_type=MESH)
        return carry

    lax.fori_loop(1, PEERS, signal, 0)
    for step in (-1, 1):
        pl.semaphore_signal(barrier, inc=1, device_id=z_neighbour(*here, step), device_id_type=MESH)
    pl.semaphore_wait(barrier, PEERS + 1)


def slot_of(name, half):
    if not isinstance(name, str):
        return name
    k = int(name[1])
    if name.endswith("x") or name[0] == "s":
        return half * 4 + k
    return (1 - half) * 4 + k


def out_kernel(parts_ref, slots_out, slots, plane_send, plane_recv, ring_send, ring_recv, keep_sem):
    here = place()
    column, half, core, zl = here
    me = column * 2 + core
    own = half * 4 + zl
    greet(here)

    for which, (part, slot) in enumerate(((1 - half, OUT), (half, own))):

        def send(ahead, carry, which=which, part=part, slot=slot):
            peer, target = plane_peer(*here, ahead)
            pltpu.make_async_remote_copy(
                src_ref=parts_ref.at[part, peer],
                dst_ref=slots.at[slot, :, :, me],
                send_sem=plane_send.at[which],
                recv_sem=plane_recv.at[which],
                device_id=target,
                device_id_type=MESH,
            ).start()
            return carry

        lax.fori_loop(1, PEERS, send, 0)
        pltpu.make_async_copy(
            parts_ref.at[part, me], slots.at[slot, :, :, me], plane_recv.at[which]
        ).start()
    wait_for(slots.at[OUT], plane_recv.at[0])
    wait_for(slots.at[own], plane_recv.at[1])

    targets = (z_neighbour(*here, -1), z_neighbour(*here, 1))
    for case in range(4):

        @pl.when(zl == case)
        def _(case=case):
            lists = (LEFT[case], RIGHT[case])
            waited = {"s" + str(case)}
            sends = []
            names = ["s0", "s1", "s2", "s3", "c0", "c1", "c2", "c3"]
            if case in (0, 3):
                names.append(PASS)
            for turn in range(max(len(items) for items in lists)):
                for way in (0, 1):
                    if turn >= len(lists[way]):
                        continue
                    source, goal = lists[way][turn]
                    at = slot_of(source, half)
                    if source != OUT and source not in waited:
                        wait_for(slots.at[at], ring_recv.at[at])
                        waited.add(source)
                    to = slot_of(goal, half)
                    copy = pltpu.make_async_remote_copy(
                        src_ref=slots.at[at],
                        dst_ref=slots.at[to],
                        send_sem=ring_send.at[way, turn],
                        recv_sem=ring_recv.at[to],
                        device_id=targets[way],
                        device_id_type=MESH,
                    )
                    copy.start()
                    sends.append(copy)
            for name in names:
                if name not in waited:
                    at = slot_of(name, half)
                    wait_for(slots.at[at], ring_recv.at[at])
            for copy in sends:
                copy.wait_send()

    keep = pltpu.make_async_copy(slots.at[pl.ds(0, PLANES)], slots_out, keep_sem)
    keep.start()
    keep.wait()
    for which in (0, 1):
        wait_for(parts_ref.at[which, pl.ds(0, PEERS - 1)], plane_send.at[which])


def back_kernel(
    sums_ref, got_out, got, from_left, from_right, final, ring_send, left_recv, right_recv, plane_send, plane_recv, keep_sem
):
    here = place()
    column, half, core, zl = here
    me = column * 2 + core
    greet(here)
    targets = (z_neighbour(*here, -1), z_neighbour(*here, 1))

    def add(ref, at, plane):
        ref[at] = (ref[at].astype(jnp.float32) + sums_ref[plane].astype(jnp.float32)).astype(jnp.bfloat16)

    for case in range(4):

        @pl.when(zl == case)
        def _(case=case):
            lists = (BACK_LEFT[case], BACK_RIGHT[case])
            buffers = (from_right, from_left)
            arrived = (right_recv, left_recv)
            sends = []
            for turn in range(max(len(items) for items in lists)):
                for way in (0, 1):
                    if turn >= len(lists[way]):
                        continue
                    item = lists[way][turn]
                    into, recv = buffers[way], arrived[way]
                    starts = case == (3, 0)[way]
                    ends = case == (0, 3)[way]
                    if item[0] == "p":
                        at = half * 4 + int(item[1])
                        wait_for(into.at[at], recv.at[at])
                        source, to = into.at[at], PLANES
                    else:
                        at = slot_of(item, half)
                        to = at
                        if starts:
                            source = sums_ref.at[at]
                        else:
                            wait_for(into.at[at], recv.at[at])
                            add(into, at, at)
                            source = into.at[at]
                    copy = pltpu.make_async_remote_copy(
                        src_ref=source,
                        dst_ref=into.at[to],
                        send_sem=ring_send.at[way, turn],
                        recv_sem=recv.at[to],
                        device_id=targets[way],
                        device_id_type=MESH,
                    )
                    copy.start()
                    sends.append(copy)
            own = half * 4 + case
            total = sums_ref[own].astype(jnp.float32)
            if case > 0:
                wait_for(from_left.at[own], left_recv.at[own])
                total = total + from_left[own].astype(jnp.float32)
            if case < 3:
                wait_for(from_right.at[own], right_recv.at[own])
                total = total + from_right[own].astype(jnp.float32)
            final[half] = total.astype(jnp.bfloat16)
            into, recv = (from_left, left_recv) if case < 2 else (from_right, right_recv)
            at = PLANES if case in (1, 2) else own
            wait_for(into.at[at], recv.at[at])
            final[1 - half] = into[at]
            for copy in sends:
                copy.wait_send()

    def send(ahead, carry):
        peer, target = plane_peer(*here, ahead)
        pltpu.make_async_remote_copy(
            src_ref=final.at[:, :, peer],
            dst_ref=got.at[me],
            send_sem=plane_send,
            recv_sem=plane_recv,
            device_id=target,
            device_id_type=MESH,
        ).start()
        return carry

    lax.fori_loop(1, PEERS, send, 0)
    pltpu.make_async_copy(final.at[:, :, me], got.at[me], plane_recv).start()
    wait_for(got, plane_recv)
    keep = pltpu.make_async_copy(got, got_out, keep_sem)
    keep.start()
    keep.wait()
    wait_for(got.at[pl.ds(0, PEERS - 1)], plane_send)


def gelu_tanh(value):
    return 0.5 * value * (1.0 + jnp.tanh(0.7978845608 * (value + 0.044715 * value * value * value)))


def by_peer(array):
    samples, local_tok, width = array.shape
    split = array.reshape(samples, local_tok, COLUMNS, 2, 2, 2, HEAD)
    split = split.transpose(3, 2, 4, 5, 1, 6, 0)
    return split.reshape(2, PEERS, 2, local_tok * HEAD, samples)


def per_device(block_input, out_grad, norm_gain, w_in, w_out):
    own_rows, local_tok, width = block_input.shape
    gain_col = norm_gain[:, :, None]
    rows = local_tok * HEAD
    parts = jnp.stack([by_peer(block_input), by_peer(out_grad)], axis=2)
    block = (2, 2, PEERS, rows, own_rows)
    slots = pl.pallas_call(
        out_kernel,
        out_shape=jax.ShapeDtypeStruct((PLANES, *block), jnp.bfloat16),
        in_specs=[pl.BlockSpec(memory_space=pltpu.VMEM)],
        out_specs=pl.BlockSpec(memory_space=pl.ANY),
        scratch_shapes=[
            pltpu.VMEM((PLANES + 2, *block), jnp.bfloat16),
            pltpu.SemaphoreType.DMA((2,)),
            pltpu.SemaphoreType.DMA((2,)),
            pltpu.SemaphoreType.DMA((2, 6)),
            pltpu.SemaphoreType.DMA((PLANES + 2,)),
            pltpu.SemaphoreType.DMA,
        ],
        compiler_params=pltpu.CompilerParams(
            collective_id=0, has_side_effects=True, vmem_limit_bytes=40 * 2**20
        ),
    )(parts)
    slots = slots.reshape(2, 4, 2, 2, COLUMNS, 2 * rows, own_rows)
    slots = slots.transpose(2, 3, 4, 0, 5, 1, 6).reshape(2, 2, width, 4 * own_rows)
    mixed_all, dmix_all = slots[0], slots[1]
    mixed_f = mixed_all.astype(jnp.float32)
    scale = lax.rsqrt(jnp.mean(mixed_f * mixed_f, axis=1, keepdims=True) + EPS)
    normed_all = (mixed_f * scale * gain_col).astype(jnp.bfloat16)
    pre = jnp.einsum("tdb,tdf->tbf", normed_all, w_in, preferred_element_type=jnp.float32)
    act, pull = jax.vjp(gelu_tanh, pre)
    act_b = act.astype(jnp.bfloat16)
    act_grad = jnp.einsum("tdb,tfd->tbf", dmix_all, w_out, preferred_element_type=jnp.float32)
    pre_grad = pull(act_grad)[0].astype(jnp.bfloat16)
    partial_grad = jnp.einsum("tbf,tdf->tdb", pre_grad, w_in, preferred_element_type=jnp.float32)
    upper = partial_grad * gain_col
    inner = jnp.sum(upper * mixed_f, axis=1, keepdims=True)
    back = (scale * upper - mixed_f * scale * scale * scale * inner / WIDTH).astype(jnp.bfloat16)
    back = back.reshape(2, COLUMNS, 2, 2 * rows, 4, own_rows).transpose(2, 4, 0, 1, 3, 5)
    back = back.reshape(PLANES, 2, PEERS, rows, own_rows)
    got = pl.pallas_call(
        back_kernel,
        out_shape=jax.ShapeDtypeStruct((PEERS, 2, 2, rows, own_rows), jnp.bfloat16),
        in_specs=[pl.BlockSpec(memory_space=pltpu.VMEM)],
        out_specs=pl.BlockSpec(memory_space=pl.ANY),
        scratch_shapes=[
            pltpu.VMEM((PEERS, 2, 2, rows, own_rows), jnp.bfloat16),
            pltpu.VMEM((PLANES + 1, 2, PEERS, rows, own_rows), jnp.bfloat16),
            pltpu.VMEM((PLANES + 1, 2, PEERS, rows, own_rows), jnp.bfloat16),
            pltpu.VMEM((2, 2, PEERS, rows, own_rows), jnp.bfloat16),
            pltpu.SemaphoreType.DMA((2, 6)),
            pltpu.SemaphoreType.DMA((PLANES + 1,)),
            pltpu.SemaphoreType.DMA((PLANES + 1,)),
            pltpu.SemaphoreType.DMA,
            pltpu.SemaphoreType.DMA,
            pltpu.SemaphoreType.DMA,
        ],
        compiler_params=pltpu.CompilerParams(
            collective_id=1, has_side_effects=True, vmem_limit_bytes=40 * 2**20
        ),
    )(back)
    grad_out = jnp.einsum(
        "tbf,tdb->tfd", act_b, dmix_all, preferred_element_type=jnp.float32
    ).astype(jnp.bfloat16)
    grad_in = jnp.einsum(
        "tdb,tbf->tdf", normed_all, pre_grad, preferred_element_type=jnp.float32
    ).astype(jnp.bfloat16)
    got = got.reshape(COLUMNS, 2, 2, 2, local_tok, HEAD, own_rows).transpose(6, 4, 0, 2, 1, 3, 5)
    returned = got.reshape(own_rows, local_tok, width)
    input_grad = (out_grad.astype(jnp.float32) + returned.astype(jnp.float32)).astype(jnp.bfloat16)
    return (input_grad, grad_in, grad_out)


def solution(mesh):
    in_specs = (
        P("hid", "tok", None),
        P("hid", "tok", None),
        P("tok", None),
        P("tok", None, "hid"),
        P("tok", "hid", None),
    )
    out_specs = (P("hid", "tok", None), P("tok", None, "hid"), P("tok", "hid", None))
    return jax.shard_map(
        per_device, mesh=mesh, in_specs=in_specs, out_specs=out_specs, check_vma=False
    )
```

time: 363 us -> 270 us (0.74)
  waiting for transfers between devices: 270 us -> 0 us
  Pallas kernels: 0 us -> 199 us
  starting transfers between devices: 34.5 us -> 0 us
  local copies, waits for them, and re-layouts: 21.3 us -> 35.5 us
  between operations: 13.9 us -> 0.77 us
  matrix products: 16.7 us -> 24.8 us
    pallas_call x0 -> x2, Pallas kernels: none -> 199 us  [the longest x1 108 us: per_device(): pl.pallas_call(back_kernel, out_shape=jax.ShapeDtypeStruct((PEERS, 2, 2,...]
    all_gather x2 -> x0, waiting for transfers between devices: 137 us -> none  [the longest x1 79.7 us: per_device(): lax.all_gather(out_grad, 'hid', axis=0, tiled=True)]
    reduce_scatter x1 -> x0, waiting for transfers between devices: 74.3 us -> none  [per_device(): lax.psum_scatter(partial_grad, 'hid', scatter_dimension=2, tiled=True)]
    all_to_all x3 -> x0, waiting for transfers between devices: 58.9 us -> none  [the longest x1 48.6 us: per_device(): lax.all_to_all(head_major(all_grad), 'tok', split_axis=0, concat_axis=1,...]
    all_to_all x3 -> x0, starting transfers between devices: 34.4 us -> none  [the longest x1 12.4 us: per_device(): lax.all_to_all(mixed_back.reshape(local_tok, TOKENS, HEAD, own_rows), 'to...]
    convert_element_type x1 -> x3, local copies, waits for them, and re-layouts: 1.31 us -> 14.8 us  [the longest x2 10.9 us: per_device(): mixed_f = mixed_all.astype(jnp.float32)]
    reshape x1 -> x2, local copies, waits for them, and re-layouts: 0.89 us -> 9.35 us  [the longest x1 5.4 us: per_device(): slots = slots.reshape(2, 4, 2, 2, COLUMNS, 2 * rows, own_rows)]
    mul x0 -> x1, matrix products: none -> 7.87 us  [per_device(): mixed_f * scale * scale * scale * inner / WIDTH]
  transfers between devices with their start and end apart: 6 -> 0, of which waited for: 5 -> 0; matrix products, arithmetic and copies ran while one was open for 5% -> 0% of each run, Pallas kernels for 0% -> 0%
where the time goes in v1:
time: 270 us; the launch traced here: 265 us
  Pallas kernels  199 us (74%)
  local copies, waits for them, and re-layouts  35.5 us (13%)
  matrix products  24.8 us (9%)
  other arithmetic  5.64 us (2%)
    pallas_call x1, Pallas kernels, per_device(): pl.pallas_call(back_kernel, out_shape=jax.ShapeDtypeStruct((PEERS, 2, 2,...  108 us
    pallas_call x1, Pallas kernels, per_device(): pl.pallas_call(out_kernel, out_shape=jax.ShapeDtypeStruct((PLANES, *block...  91 us
    convert_element_type x2, local copies, waits for them, and re-layouts, per_device(): mixed_f = mixed_all.astype(jnp.float32)  10.9 us
    mul x1, matrix products, per_device(): mixed_f * scale * scale * scale * inner / WIDTH  7.87 us
    dot_general x1, matrix products, per_device(): jnp.einsum('tdb,tdf->tbf', normed_all, w_in, preferred_element_type=jnp.f...  5.83 us

profile of v1, /device:TPU:1, one launch (start us, length us, event | category | flops | bytes accessed | tf_op | source)
XLA Modules:
  0.0 265.5 jit_solution(7956573952374777035)
XLA Ops:
  0.6 0.0 copy-start
  0.6 1.5 copy.17
  2.2 0.9 copy.21
  3.1 1.4 copy.18
  4.5 0.1 copy.19
  4.6 1.1 pad_maximum_fusion.parts_ref
  5.8 91.0 %shard_map.76 = bf16[8,2,2,32,16,128]{5,4,3,2,1,0:T(8,128)(2,1)S(1)} custom-call(bf16[2,32,2,2,16,128]{5,4,3,2,1,0:T(8,128)(2,1)S(1)} %pad_maximum_fusion.parts_ref), custom_call_target="tpu_custom_call" | custom-call | tf_op jit(solution)/shard_map/pallas_call | solution.py:271
  96.8 5.4 %copy.38 = bf16[2,4,2,2,16,32,128]{6,1,5,0,4,3,2:T(4,128)(2,1)S(1)} copy(bf16[2,4,2,2,16,32,128]{6,5,4,3,2,1,0:T(8,128)(2,1)S(1)} %bitcast.46) | data formatting | bytes 8388608 | tf_op jit(solution)/shard_map/reshape | solution.py:288
  102.2 1.1 multiply_reduce_fusion
  103.4 3.3 %fusion.22 = (bf16[1,2,16,2,32,4,128]{6,5,4,3,2,1,0:T(4,128)(2,1)}, f32[1,2,16,2,32,4,128]{6,5,4,3,2,1,0:T(4,128)}) fusion(bf16[2,2,16,2,32,4,128]{6,5,4,3,2,1,0:T(4,128)(2,1)S(1)} %bitcast.50), kind=kLoop, calls=%fused_computation.38 | loop fusion | flops 1048576 | bytes 10485760 | tf_op jit(solution)/shard_map/slice | solution.py:290
  106.6 4.1 %squeeze.4 = bf16[2,1024,512]{2,1,0:T(8,128)(2,1)} reshape(bf16[1,2,16,2,32,4,128]{6,5,4,3,2,1,0:T(4,128)(2,1)} %get-tuple-element.6) | data formatting | bytes 4194304 | tf_op jit(solution)/shard_map/squeeze | solution.py:290
  110.7 5.1 %fusion.23 = f32[2,512,512]{2,1,0:T(8,128)} fusion(bf16[2,1024,512]{2,1,0:T(8,128)(2,1)} %squeeze.4, bf16[2,512,1024]{2,1,0:T(8,128)(2,1)} %param.9), kind=kOutput, calls=%fused_computation.39 | convolution fusion | flops 1073741824 | bytes 6291456 | tf_op jit(solution)/shard_map/tdb,tfd->tbf/dot_general | solution.py:297
  115.9 5.5 %reshape.58 = f32[2,1024,512]{2,1,0:T(8,128)} reshape(f32[1,2,16,2,32,4,128]{6,5,4,3,2,1,0:T(4,128)} %get-tuple-element.7) | data formatting | bytes 8388608 | tf_op jit(solution)/shard_map/convert_element_type | solution.py:291
  121.3 5.4 %copy.23 = f32[2,1024,512]{1,2,0:T(8,128)} copy(f32[2,1024,512]{2,1,0:T(8,128)} %reshape.58) | data formatting | bytes 8388608 | tf_op jit(solution)/shard_map/convert_element_type | solution.py:291
  126.7 0.0 copy-done
  126.8 0.0 copy-done.4
  126.8 5.8 %fusion.6 = (bf16[2,512,512]{2,1,0:T(8,128)(2,1)S(1)}, f32[2,512,512]{2,1,0:T(8,128)S(1)}) fusion(f32[2,512,512]{2,1,0:T(8,128)} %fusion.23, bf16[2,1024,512]{2,1,0:T(8,128)(2,1)S(1)} %copy-done, f32[2,1024,512]{1,2,0:T(8,128)} %copy.23, f32[2,1024]{1,0:T(2,128)S(1)} %copy-done.4, f32[2,512]{1,0:T(2,128)S(1)} %bitcast.56), kind=kOutput, calls=%fused_computation.15 | convolution fusion | flops 1089470464 | bytes 11546624 | tf_op jit(solution)/shard_map/tdb,tdf->tbf/dot_general | solution.py:294
  132.6 0.0 copy-start.3
  132.6 0.0 copy-done.2
  132.6 0.0 copy-start.1
  132.6 3.2 %convolution_convert_fusion = bf16[2,512,1024]{2,1,0:T(8,128)(2,1)} fusion(bf16[2,1024,512]{2,1,0:T(8,128)(2,1)S(1)} %copy-done.2, f32[2,512,512]{2,1,0:T(8,128)S(1)} %get-tuple-element.9), kind=kOutput, calls=%fused_computation.21 | convolution fusion | flops 1079508992 | bytes 6291456 | tf_op jit(solution)/shard_map/tbf,tdb->tfd/dot_general | solution.py:326
  135.8 0.0 copy-done.3
  135.8 0.0 copy-done.1
  135.8 2.8 %convolution_convert_fusion.1 = bf16[2,1024,512]{2,1,0:T(8,128)(2,1)} fusion(bf16[2,512,512]{2,1,0:T(8,128)(2,1)S(1)} %get-tuple-element.8, f32[2,1024,512]{1,2,0:T(8,128)S(1)} %copy-done.1, f32[2,1024]{1,0:T(2,128)S(1)} %copy-done.4, f32[2,512]{1,0:T(2,128)S(1)} %bitcast.57), kind=kOutput, calls=%fused_computation.22 | convolution fusion | flops 1077936128 | bytes 7352320 | tf_op jit(solution)/shard_map/tdb,tbf->tdf/dot_general | solution.py:329
  138.6 7.9 %fusion.2 = bf16[2,1024,512]{1,2,0:T(8,128)(2,1)} fusion(f32[2,1024,512]{1,2,0:T(8,128)} %copy.23, f32[2,1024]{1,0:T(2,128)S(1)} %copy-done.4, f32[2,512]{1,0:T(2,128)S(1)} %bitcast.58, bf16[2,512,512]{2,1,0:T(8,128)(2,1)} %copy-done.3, bf16[2,1024,512]{2,1,0:T(8,128)(2,1)S(1)} %copy-done), kind=kOutput, calls=%fused_computation.4 | convolution fusion | flops 2159020032 | bytes 9449472 | tf_op jit(solution)/shard_map/mul | solution.py:302
  146.5 3.9 %copy.26 = bf16[2,1024,512]{2,1,0:T(8,128)(2,1)} copy(bf16[2,1024,512]{1,2,0:T(8,128)(2,1)} %fusion.2) | data formatting | bytes 4194304 | tf_op jit(solution)/shard_map/convert_element_type | solution.py:302
  150.4 4.0 %reshape.56 = bf16[2,16,2,32,4,128]{5,4,3,2,1,0:T(4,128)(2,1)} reshape(bf16[2,1024,512]{2,1,0:T(8,128)(2,1)} %copy.26) | data formatting | bytes 4194304 | tf_op jit(solution)/shard_map/reshape | solution.py:303
  154.4 2.0 copy.27
  156.4 107.7 %shard_map.77 = bf16[32,2,2,16,128]{4,3,2,1,0:T(8,128)(2,1)S(1)} custom-call(bf16[8,2,32,16,128]{4,3,2,1,0:T(8,128)(2,1)S(1)} %bitcast.47), custom_call_target="tpu_custom_call" | custom-call | tf_op jit(solution)/shard_map/pallas_call | solution.py:305
  264.1 0.1 copy.28
  264.2 0.1 fusion.10
  264.4 1.1 copy.31
  (4 shorter events, 0.0 us)
Async XLA Ops:
  0.6 126.1 %copy-start = (bf16[2,1024,512]{2,1,0:T(8,128)(2,1)S(1)}, bf16[2,1024,512]{2,1,0:T(8,128)(2,1)}, u32[]{:S(2)}) copy-start(bf16[2,1024,512]{2,1,0:T(8,128)(2,1)} %param.8) | copy-start | bytes 6291460
  121.3 5.4 %copy-start.4 = (f32[2,1024]{1,0:T(2,128)S(1)}, f32[2,1024]{1,0:T(2,128)}, u32[]{:S(2)}) copy-start(f32[2,1024]{1,0:T(2,128)} %param.7) | copy-start | bytes 24580
  126.8 5.9 %copy-start.2 = (bf16[2,1024,512]{2,1,0:T(8,128)(2,1)S(1)}, bf16[2,1024,512]{2,1,0:T(8,128)(2,1)}, u32[]{:S(2)}) copy-start(bf16[2,1024,512]{2,1,0:T(8,128)(2,1)} %squeeze.4) | copy-start | bytes 6291460
  132.6 3.2 %copy-start.3 = (bf16[2,512,512]{2,1,0:T(8,128)(2,1)}, bf16[2,512,512]{2,1,0:T(8,128)(2,1)S(1)}, u32[]{:S(2)}) copy-start(bf16[2,512,512]{2,1,0:T(8,128)(2,1)S(1)} %get-tuple-element.8) | copy-start | bytes 3145732
  132.6 3.2 %copy-start.1 = (f32[2,1024,512]{1,2,0:T(8,128)S(1)}, f32[2,1024,512]{1,2,0:T(8,128)}, u32[]{:S(2)}) copy-start(f32[2,1024,512]{1,2,0:T(8,128)} %copy.23) | copy-start | bytes 12582916

commit v2 on v0

v2 whole, which is shorter than its diff:
```python
import jax
import jax.numpy as jnp
from jax import lax
from jax.experimental import pallas as pl
from jax.experimental.pallas import tpu as pltpu
from jax.sharding import PartitionSpec as P

WIDTH = 1024
HEAD = 8
EPS = 1e-06
MESH = pl.DeviceIdType.MESH

COLUMNS = 16
PEERS = 32
PLANES = 8
OUT, PASS = 8, 9
DEPTH = 2
TAIL = 4

ORDER = {
    0: [
        "f.l.o.c0.1", "f.r.s0.s0.0", "f.l.p.c1.0", "f.r.c3.c3.1", "f.l.p.c1.1", "f.r.c2.c2.0", "f.r.c2.c2.1", "f.l.o.c0.0", "f.r.s0.s0.1", "m.2.1",
        "b.r.s2.1", "m.3.0", "b.r.s3.0", "f.r.c3.c3.0", "m.0.1", "b.r.c0.1", "m.1.0", "b.r.c1.0", "b.r.s1.0", "m.1.1",
        "b.r.s1.1", "b.r.c1.1", "m.0.0", "b.r.c0.0", "m.3.1", "b.r.s3.1", "m.2.0", "b.l.c2.0", "b.r.s2.0", "b.l.c2.1",
        "b.r.p1.0", "b.l.c3.1", "b.l.c3.0", "b.r.p1.1", "w.0", "e.1", "e.0", "w.1", "w.2", "w.3",
    ],
    1: [
        "f.l.o.p.0", "f.l.o.p.1", "f.r.s1.s1.0", "f.l.s1.s1.1", "f.r.s1.s1.1", "f.l.s1.s1.0", "f.r.s0.s0.0", "f.r.c3.c3.1", "f.l.s2.s2.1", "m.2.0",
        "f.l.s3.s3.0", "f.r.c2.c2.0", "f.l.c0.c0.1", "f.r.c2.c2.1", "m.1.0", "f.l.c1.c1.0", "f.r.s0.s0.1", "m.1.1", "f.l.c1.c1.1", "f.r.c3.c3.0",
        "f.l.s3.s3.1", "b.r.c1.0", "f.l.c0.c0.0", "m.3.0", "b.r.s3.0", "m.0.0", "f.l.s2.s2.0", "m.0.1", "b.r.c0.1", "b.r.c1.1",
        "b.l.c2.0", "m.2.1", "b.r.s2.1", "b.l.c2.1", "b.r.c0.0", "m.3.1", "b.l.c3.1", "w.0", "b.r.s3.1", "w.1",
        "b.l.c3.0", "b.r.s2.0", "b.l.s0.1", "w.2", "w.3", "b.l.s0.0", "e.0", "e.1",
    ],
    2: [
        "f.r.o.p.0", "f.r.o.p.1", "f.l.s2.s2.0", "f.r.s2.s2.1", "f.l.s2.s2.1", "f.r.s2.s2.0", "f.l.s3.s3.0", "f.l.c0.c0.1", "f.r.s1.s1.1", "m.1.0",
        "f.r.s0.s0.0", "f.l.c1.c1.0", "f.r.c3.c3.1", "f.l.c1.c1.1", "m.2.0", "f.r.c2.c2.0", "f.l.s3.s3.1", "m.2.1", "f.r.c2.c2.1", "f.l.c0.c0.0",
        "f.r.s0.s0.1", "b.l.c2.0", "f.r.c3.c3.0", "m.0.0", "b.l.s0.0", "m.3.0", "f.r.s1.s1.0", "m.3.1", "b.l.c3.1", "b.l.c2.1",
        "b.r.c1.0", "m.1.1", "b.l.s1.1", "b.r.c1.1", "b.l.c3.0", "m.0.1", "b.r.c0.1", "w.0", "b.l.s0.1", "w.1",
        "b.r.c0.0", "b.l.s1.0", "b.r.s3.1", "w.2", "w.3", "b.r.s3.0", "e.0", "e.1",
    ],
    3: [
        "f.r.o.c3.1", "f.l.s3.s3.0", "f.r.p.c2.0", "f.l.c0.c0.1", "f.r.p.c2.1", "f.l.c1.c1.0", "f.l.c1.c1.1", "f.r.o.c3.0", "f.l.s3.s3.1", "m.1.1",
        "b.l.s1.1", "m.0.0", "b.l.s0.0", "f.l.c0.c0.0", "m.3.1", "b.l.c3.1", "m.2.0", "b.l.c2.0", "b.l.s2.0", "m.2.1",
        "b.l.s2.1", "b.l.c2.1", "m.3.0", "b.l.c3.0", "m.0.1", "b.l.s0.1", "m.1.0", "b.r.c1.0", "b.l.s1.0", "b.r.c1.1",
        "b.l.p2.0", "b.r.c0.1", "b.r.c0.0", "b.l.p2.1", "w.0", "e.1", "e.0", "w.1", "w.2", "w.3",
    ],
}


def place():
    tok, zl = lax.axis_index("tok"), lax.axis_index("hid")
    core, half, column = lax.rem(tok, 2), lax.rem(tok // 2, 2), tok // 4
    return column, half, core, zl


def device(column, half, core, zl):
    return (column * 4 + half * 2 + core, zl)


def z_neighbour(column, half, core, zl, step):
    z = lax.rem(half * 4 + zl + PLANES + step, PLANES)
    return device(column, z // 4, core, lax.rem(z, 4))


def plane_peer(column, half, core, zl, ahead):
    peer = lax.rem(column * 2 + core + ahead, PEERS)
    return peer, device(peer // 2, half, lax.rem(peer, 2), zl)


def wait_for(ref, sem):
    pltpu.make_async_copy(ref, ref, sem).wait()


def dot(left, right, dims):
    return lax.dot_general(left, right, (dims, ((), ())), preferred_element_type=jnp.float32)


def steps_of(case):
    parts, mlps, now = [], [], []
    here = set()
    sent = {"l": [], "r": []}

    def arrive(name, head):
        if (name, head) not in here:
            here.add((name, head))
            kind = {"o": "out", f"s{case}": "own"}.get(name, "arrived")
            now.append((kind, name, int(head)))

    for item in ORDER[case]:
        item = item.split(".")
        if item[0] in "mw":
            if item[0] == "m":
                mlps.append((int(item[1]), int(item[2])))
                arrive("s" + item[1], item[2])
                arrive("c" + item[1], item[2])
            parts.append(now)
            now = []
            continue
        if item[0] == "e":
            now.append(("end", int(item[1])))
            continue
        if item[0] == "f":
            arrive(item[2], item[-1])
        turns = sent[item[1]]
        late = len(turns) - DEPTH
        if late >= 0:
            now.append(("sent", turns[late], item[1], late))
        now.append((item[0], *item[1:-1], int(item[-1]), len(turns)))
        turns.append(item[0])
        if len(sent["l"]) + len(sent["r"]) == 3:
            now.append(("prepare",))
    parts.append(now)
    for way, turns in sent.items():
        parts[-1] += [("sent", turns[late], way, late) for late in range(max(0, len(turns) - DEPTH), len(turns))]
    return parts, mlps


def kernel(
    input_ref, cotangent_ref, gain_ref, w_in_ref, w_out_ref, returned_ref, grad_in, grad_out,
    parts, gain, slots, sums, from_left, from_right, final, got, w_in, w_in_t, w_out, normed, cotangent, act, pre_grad,
    plane_send, plane_recv, ring_send, ring_recv, left_recv, right_recv, back_send, back_recv, weight_sem,
):
    here = place()
    column, half, core, zl = here
    me = column * 2 + core
    own = half * 4 + zl
    load_in = pltpu.make_async_copy(w_in_ref, w_in, weight_sem.at[0])
    load_out = pltpu.make_async_copy(w_out_ref, w_out, weight_sem.at[1])
    load_in.start()
    load_out.start()

    barrier = pltpu.get_barrier_semaphore()

    def signal(ahead, carry):
        _, target = plane_peer(*here, ahead)
        pl.semaphore_signal(barrier, inc=1, device_id=target, device_id_type=MESH)
        return carry

    lax.fori_loop(1, PEERS, signal, 0)
    for step in (-1, 1):
        pl.semaphore_signal(barrier, inc=1, device_id=z_neighbour(*here, step), device_id_type=MESH)

    for which, ref in enumerate((input_ref, cotangent_ref)):
        tokens = [ref[token].astype(jnp.float32).reshape(COLUMNS, 2, 2, 2, HEAD, 128) for token in range(2)]
        for to_half, to_core, head in ((a, b, c) for a in range(2) for b in range(2) for c in range(2)):
            both = jnp.stack([token[:, to_half, to_core, head] for token in tokens], axis=1)
            parts[to_half, head, :, to_core, which] = both.reshape(COLUMNS, 2 * HEAD, 128).astype(jnp.bfloat16)
    pl.semaphore_wait(barrier, PEERS + 1)

    phases = [(1 - half, OUT, 0), (1 - half, OUT, 1), (half, own, 0), (half, own, 1)]
    for which, (part, slot, head) in enumerate(phases):

        def send(ahead, carry, which=which, part=part, slot=slot, head=head):
            peer, target = plane_peer(*here, ahead)
            pltpu.make_async_remote_copy(
                src_ref=parts.at[part, head, peer // 2, lax.rem(peer, 2)],
                dst_ref=slots.at[slot, head, :, me],
                send_sem=plane_send.at[which],
                recv_sem=plane_recv.at[which],
                device_id=target,
                device_id_type=MESH,
            ).start()
            return carry

        lax.fori_loop(1, PEERS, send, 0)
        pltpu.make_async_copy(
            parts.at[part, head, column, core], slots.at[slot, head, :, me], plane_recv.at[which]
        ).start()

    def prepare():
        load_in.wait()
        load_out.wait()

        def turn(at, carry):
            token, chunk = at // 4, lax.rem(at, 4)
            rows = pl.ds(pl.multiple_of(chunk * 256, 256), 256)
            w_in_t[token, :, rows] = w_in[token, rows, :].T
            return carry

        lax.fori_loop(0, 8, turn, 0)
        for token in range(2):
            wide = jnp.broadcast_to(gain_ref[token : token + 1, :], (128, WIDTH)).T
            gain[token] = wide.reshape(COLUMNS, 2, 32, 128)

    targets = {"l": z_neighbour(*here, -1), "r": z_neighbour(*here, 1)}
    buffers = {"l": from_right, "r": from_left}
    arrivals = {"l": right_recv, "r": left_recv}

    def plane_of(name):
        k = int(name[1])
        return (1 - half) * 4 + k if name[0] == "c" else half * 4 + k

    def slot_of(name):
        return {"o": OUT, "p": PASS}.get(name) if name in "op" else plane_of(name)

    def end(case, head):
        total = sums[own, head].astype(jnp.float32)
        if case > 0:
            wait_for(from_left.at[own, head], left_recv.at[own, head])
            total = total + from_left[own, head].astype(jnp.float32)
        if case < 3:
            wait_for(from_right.at[own, head], right_recv.at[own, head])
            total = total + from_right[own, head].astype(jnp.float32)
        final[head, half] = total.astype(jnp.bfloat16)
        into, recv = (from_left, left_recv) if case < 2 else (from_right, right_recv)
        at = PLANES if case in (1, 2) else own
        wait_for(into.at[at, head], recv.at[at, head])
        final[head, 1 - half] = into[at, head]

        def send(ahead, carry):
            peer, target = plane_peer(*here, ahead)
            pltpu.make_async_remote_copy(
                src_ref=final.at[head, :, peer],
                dst_ref=got.at[head, me],
                send_sem=back_send.at[head],
                recv_sem=back_recv.at[head],
                device_id=target,
                device_id_type=MESH,
            ).start()
            return carry

        lax.fori_loop(1, PEERS, send, 0)
        pltpu.make_async_copy(final.at[head, :, me], got.at[head, me], back_recv.at[head]).start()

    def run(case, ops):
        for op in ops:
            if op[0] == "prepare":
                prepare()
                continue
            if op[0] == "end":
                end(case, op[1])
                continue
            if op[0] == "arrived":
                at, head = slot_of(op[1]), op[2]
                wait_for(slots.at[at, head], ring_recv.at[at, head])
                continue
            if op[0] in ("out", "own"):
                at, head = slot_of(op[1]), op[2]
                wait_for(slots.at[at, head], plane_recv.at[head + 2 * (op[0] == "own")])
                continue
            if op[0] == "sent":
                ref = slots.at[0, 0] if op[1] == "f" else sums.at[0, 0]
                wait_for(ref, ring_send.at["lr".index(op[2]), op[3]])
                continue
            way, name, head, turn = op[1], op[2], op[-2], op[-1]
            if op[0] == "f":
                at = slot_of(name)
                crosses = case == {"l": 0, "r": 3}[way]
                to = half * 4 + int(op[3][1]) if crosses else slot_of(op[3])
                from_ref, to_ref, recv = slots.at[at, head], slots.at[to, head], ring_recv.at[to, head]
            else:
                into, arrived = buffers[way], arrivals[way]
                at = to = plane_of(name)
                if name[0] == "p":
                    wait_for(into.at[at, head], arrived.at[at, head])
                    from_ref, to = into.at[at, head], PLANES
                elif case == {"l": 3, "r": 0}[way]:
                    from_ref = sums.at[at, head]
                else:
                    wait_for(into.at[at, head], arrived.at[at, head])
                    total = into[at, head].astype(jnp.float32) + sums[at, head].astype(jnp.float32)
                    into[at, head] = total.astype(jnp.bfloat16)
                    from_ref = into.at[at, head]
                to_ref, recv = into.at[to, head], arrived.at[to, head]
            pltpu.make_async_remote_copy(
                src_ref=from_ref,
                dst_ref=to_ref,
                send_sem=ring_send.at["lr".index(way), turn],
                recv_sem=recv,
                device_id=targets[way],
                device_id_type=MESH,
            ).start()

    plans = {case: steps_of(case) for case in range(4)}
    mlps = len(plans[0][1])

    def ahead_of(step, first, count):
        for case in range(4):

            @pl.when(zl == case)
            def _(case=case):
                for at in range(first, first + count):

                    @pl.when(step == at)
                    def _(at=at):
                        run(case, plans[case][0][at])

    def mlp(step, code):
        ahead_of(step, 0, mlps)
        k, head = lax.rem(code, 8) // 2, lax.rem(code, 2)
        columns = pl.ds(pl.multiple_of(k * 128, 128), 128)

        def mixed(zs):
            return slots[zs * 4 + k, head, 0].astype(jnp.float32).reshape(512, 128)

        squares = sum(jnp.sum(mixed(zs) ** 2, axis=0, keepdims=True) for zs in range(2))
        scale = lax.rsqrt(squares / WIDTH + EPS)
        for zs in range(2):
            value = (mixed(zs) * scale * gain[head, :, zs].reshape(512, 128)).astype(jnp.bfloat16)
            normed[head, :, zs, :, columns] = value.reshape(COLUMNS, 32, 128)
            cotangent[head, :, zs, :, columns] = slots[zs * 4 + k, head, 1].reshape(COLUMNS, 32, 128)
        plain = (((1,), (0,)))
        pre = dot(w_in_t[head], normed[head, :, :, :, columns].reshape(WIDTH, 128), plain)
        act_grad = dot(w_out[head], cotangent[head, :, :, :, columns].reshape(WIDTH, 128), plain)
        squared = pre * pre
        bend = jnp.tanh(0.7978845608 * (pre + 0.044715 * squared * pre))
        half_up = 0.5 * (1.0 + bend)
        act[head, :, columns] = (pre * half_up).astype(jnp.bfloat16)
        slope = half_up + 0.5 * pre * (1.0 - bend * bend) * (0.7978845608 * (1.0 + 0.134145 * squared))
        grad = (act_grad * slope).astype(jnp.bfloat16)
        pre_grad[head, :, columns] = grad
        upper = dot(w_in[head], grad, plain).reshape(COLUMNS, 2, 32, 128)
        upper = [upper[:, zs].reshape(512, 128) * gain[head, :, zs].reshape(512, 128) for zs in range(2)]
        inner = sum(jnp.sum(upper[zs] * mixed(zs), axis=0, keepdims=True) for zs in range(2))
        factor = scale * scale * scale * inner / WIDTH
        for zs in range(2):
            back = scale * upper[zs] - mixed(zs) * factor
            sums[zs * 4 + k, head] = back.astype(jnp.bfloat16).reshape(PEERS, 16, 128)
        return code // 8

    code = jnp.int32(0)
    for case in range(4):
        packed = sum((k * 2 + head) * 8**at for at, (k, head) in enumerate(plans[case][1]))
        code = jnp.where(zl == case, jnp.int32(packed), code)
    lax.fori_loop(0, mlps, mlp, code)

    def piece(step, carry):
        ahead_of(step + mlps, mlps, TAIL)
        head, part = step // 2, lax.rem(step, 2)
        turned = ((1,), (1,))
        rows = pl.ds(pl.multiple_of(part * 256, 256), 256)
        value = dot(act[head, rows, :], cotangent[head].reshape(WIDTH, 512), turned)
        grad_out[head, rows, :] = value.astype(jnp.bfloat16)
        groups = normed[head, pl.ds(part * 8, 8)].reshape(512, 512)
        rows = pl.ds(pl.multiple_of(part * 512, 512), 512)
        grad_in[head, rows, :] = dot(groups, pre_grad[head], turned).astype(jnp.bfloat16)
        return carry

    lax.fori_loop(0, TAIL, piece, 0)
    for case in range(4):

        @pl.when(zl == case)
        def _(case=case):
            run(case, plans[case][0][mlps + TAIL])

    for which in range(len(phases)):
        wait_for(got.at[0, pl.ds(0, PEERS - 1)], plane_send.at[which])
    for head in range(2):
        wait_for(got.at[head], back_recv.at[head])
    for from_half, from_core in ((a, b) for a in range(2) for b in range(2)):
        pair = []
        for head in range(2):
            rows = got[head, :, from_half].reshape(COLUMNS, 2, 2 * HEAD, 128)[:, from_core]
            pair.append(rows.astype(jnp.float32).reshape(COLUMNS, 2, HEAD, 128))
        for token in range(2):
            both = jnp.stack([rows[:, token] for rows in pair], axis=1).reshape(COLUMNS, 2 * HEAD, 128)
            returned_ref[token, :, from_half, from_core] = both.astype(jnp.bfloat16)
    for head in range(2):
        wait_for(got.at[head, pl.ds(0, PEERS - 1)], back_send.at[head])


def per_device(block_input, out_grad, norm_gain, w_in, w_out):
    own_rows, local_tok, width = block_input.shape
    rows = local_tok * HEAD
    hidden = w_in.shape[2]
    bf16 = jnp.bfloat16
    block = (PEERS, rows, own_rows)
    anywhere = pl.BlockSpec(memory_space=pl.ANY)
    inside = pl.BlockSpec(memory_space=pltpu.VMEM)
    dma = pltpu.SemaphoreType.DMA
    turned = out_grad.transpose(1, 2, 0)
    returned, grad_in, grad_out = pl.pallas_call(
        kernel,
        out_shape=(
            jax.ShapeDtypeStruct((local_tok, COLUMNS, 2, 2, rows, own_rows), bf16),
            jax.ShapeDtypeStruct(w_in.shape, bf16),
            jax.ShapeDtypeStruct(w_out.shape, bf16),
        ),
        in_specs=[inside, inside, inside, anywhere, anywhere],
        out_specs=(inside, inside, inside),
        scratch_shapes=[
            pltpu.VMEM((2, 2, COLUMNS, 2, 2, rows, own_rows), bf16),
            pltpu.VMEM((2, COLUMNS, 2, 2 * rows, own_rows), jnp.float32),
            pltpu.VMEM((PLANES + 2, 2, 2, *block), bf16),
            pltpu.VMEM((PLANES, 2, *block), bf16),
            pltpu.VMEM((PLANES + 1, 2, *block), bf16),
            pltpu.VMEM((PLANES + 1, 2, *block), bf16),
            pltpu.VMEM((2, 2, *block), bf16),
            pltpu.VMEM((2, PEERS, 2, rows, own_rows), bf16),
            pltpu.VMEM((2, width, hidden), bf16),
            pltpu.VMEM((2, hidden, width), bf16),
            pltpu.VMEM((2, hidden, width), bf16),
            pltpu.VMEM((2, COLUMNS, 2, 2 * rows, 4 * own_rows), bf16),
            pltpu.VMEM((2, COLUMNS, 2, 2 * rows, 4 * own_rows), bf16),
            pltpu.VMEM((2, hidden, 4 * own_rows), bf16),
            pltpu.VMEM((2, hidden, 4 * own_rows), bf16),
            dma((4,)),
            dma((4,)),
            dma((2, 24)),
            dma((PLANES + 2, 2)),
            dma((PLANES + 1, 2)),
            dma((PLANES + 1, 2)),
            dma((2,)),
            dma((2,)),
            dma((2,)),
        ],
        compiler_params=pltpu.CompilerParams(
            collective_id=0, has_side_effects=True, vmem_limit_bytes=46 * 2**20
        ),
    )(block_input.transpose(1, 2, 0), turned, norm_gain, w_in, w_out)
    returned = returned.reshape(local_tok, width, own_rows)
    input_grad = (turned.astype(jnp.float32) + returned.astype(jnp.float32)).astype(jnp.bfloat16)
    return (input_grad.transpose(2, 0, 1), grad_in, grad_out)


def solution(mesh):
    in_specs = (
        P("hid", "tok", None),
        P("hid", "tok", None),
        P("tok", None),
        P("tok", None, "hid"),
        P("tok", "hid", None),
    )
    out_specs = (P("hid", "tok", None), P("tok", None, "hid"), P("tok", "hid", None))
    return jax.shard_map(
        per_device, mesh=mesh, in_specs=in_specs, out_specs=out_specs, check_vma=False
    )
```

time: 363 us -> 123 us (0.34)
  waiting for transfers between devices: 270 us -> 0 us
  Pallas kernels: 0 us -> 111 us
  starting transfers between devices: 34.5 us -> 0 us
  matrix products: 16.7 us -> 0 us
  between operations: 13.9 us -> 0.69 us
  local copies, waits for them, and re-layouts: 21.3 us -> 11.5 us
  other arithmetic: 5.02 us -> 0.17 us
    all_gather x2 -> x0, waiting for transfers between devices: 137 us -> none  [the longest x1 79.7 us: per_device(): lax.all_gather(out_grad, 'hid', axis=0, tiled=True)]
    pallas_call x0 -> x1, Pallas kernels: none -> 111 us  [per_device(): pl.pallas_call(kernel, out_shape=(jax.ShapeDtypeStruct((local_tok, COLUMN...]
    reduce_scatter x1 -> x0, waiting for transfers between devices: 74.3 us -> none  [per_device(): lax.psum_scatter(partial_grad, 'hid', scatter_dimension=2, tiled=True)]
    all_to_all x3 -> x0, waiting for transfers between devices: 58.9 us -> none  [the longest x1 48.6 us: per_device(): lax.all_to_all(head_major(all_grad), 'tok', split_axis=0, concat_axis=1,...]
    all_to_all x3 -> x0, starting transfers between devices: 34.4 us -> none  [the longest x1 12.4 us: per_device(): lax.all_to_all(mixed_back.reshape(local_tok, TOKENS, HEAD, own_rows), 'to...]
    dot_general x5 -> x0, matrix products: 16.7 us -> none  [the longest x1 4.63 us: per_device(): jnp.einsum('tdb,tbf->tdf', normed_all, pre_grad, preferred_element_type=j...]
    transpose x2 -> x0, local copies, waits for them, and re-layouts: 6.46 us -> none  [head_major(): return array.reshape(samples, local_tok, TOKENS, HEAD).transpose(2, 1, 3, 0)]
    unnamed x24 -> x17, local copies, waits for them, and re-layouts: 6.47 us -> 11.5 us
  transfers between devices with their start and end apart: 6 -> 0, of which waited for: 5 -> 0; matrix products, arithmetic and copies ran while one was open for 5% -> 0% of each run, Pallas kernels for 0% -> 0%
where the time goes in v2:
time: 123 us
  Pallas kernels  111 us (90%)
  local copies, waits for them, and re-layouts  11.5 us (9%)
    pallas_call x1, Pallas kernels, per_device(): pl.pallas_call(kernel, out_shape=(jax.ShapeDtypeStruct((local_tok, COLUMN...  111 us
    unnamed x17, local copies, waits for them, and re-layouts  11.5 us

profile of v2, /device:TPU:1, one launch (start us, length us, event | category | flops | bytes accessed | tf_op | source)
XLA Modules:
  0.0 122.9 jit_solution(2345525484025865888)
XLA Ops:
  0.6 0.0 copy-start
  0.6 1.5 %copy.8 = bf16[128,2,1024]{0,2,1:T(8,128)(2,1)S(1)} copy(bf16[128,2,1024]{2,1,0:T(2,128)(2,1)} %param.6) | data formatting | bytes 1048576 | tf_op args[1]
  2.2 1.4 %copy.9 = bf16[128,2,1024]{0,2,1:T(8,128)(2,1)S(1)} copy(bf16[128,2,1024]{2,1,0:T(2,128)(2,1)} %param.5) | data formatting | bytes 1048576 | tf_op args[0]
  3.6 0.0 copy-done
  3.6 0.0 copy-start.5
  3.6 0.7 copy-done.5
  4.3 110.5 %shard_map.76 = (bf16[2,16,2,2,16,128]{5,4,3,2,1,0:T(8,128)(2,1)S(1)}, bf16[2,1024,512]{2,1,0:T(8,128)(2,1)S(1)}, bf16[2,512,1024]{2,1,0:T(8,128)(2,1)S(1)}) custom-call(bf16[2,1024,128]{2,1,0:T(8,128)(2,1)S(1)} %bitcast.9, bf16[2,1024,128]{2,1,0:T(8,128)(2,1)S(1)} %bitcast.8, f32[2,1024]{1,0:T(2,128)S(1)} %copy-done.5, bf16[2,1024,512]{2,1,0:T(8,128)(2,1)S(1)} %copy-done, ...), custom_call_target="tpu_custom_call" | custom-call | tf_op jit(solution)/shard_map/pallas_call | solution.py:372
  114.8 0.0 copy-start.1
  114.8 1.3 %copy-done.1 = bf16[2,512,1024]{2,1,0:T(8,128)(2,1)} copy-done((bf16[2,512,1024]{2,1,0:T(8,128)(2,1)}, bf16[2,512,1024]{2,1,0:T(8,128)(2,1)S(1)}, u32[]{:S(2)}) %copy-start.1) | copy-done | bytes 2097176
  116.2 0.0 copy-start.3
  116.2 1.3 %copy-done.3 = bf16[2,1024,512]{2,1,0:T(8,128)(2,1)} copy-done((bf16[2,1024,512]{2,1,0:T(8,128)(2,1)}, bf16[2,1024,512]{2,1,0:T(8,128)(2,1)S(1)}, u32[]{:S(2)}) %copy-start.3) | copy-done | bytes 2097176
  117.5 0.0 copy-start.4
  117.5 0.2 fusion.1
  117.7 1.1 copy.10
  118.8 0.5 copy-done.4
  119.3 0.0 copy-start.2
  119.3 1.3 %copy.13 = bf16[2,1024,512]{2,1,0:T(8,128)(2,1)} copy(bf16[2,1024,512]{2,1,0:T(8,128)(2,1)S(1)} %copy-done.4) | data formatting | bytes 4194304
  120.6 1.0 copy-done.2
  121.6 1.3 %copy.14 = bf16[2,512,1024]{2,1,0:T(8,128)(2,1)} copy(bf16[2,512,1024]{2,1,0:T(8,128)(2,1)S(1)} %copy-done.2) | data formatting | bytes 4194304
Async XLA Ops:
  0.6 2.9 %copy-start = (bf16[2,1024,512]{2,1,0:T(8,128)(2,1)S(1)}, bf16[2,1024,512]{2,1,0:T(8,128)(2,1)}, u32[]{:S(2)}) copy-start(bf16[2,1024,512]{2,1,0:T(8,128)(2,1)} %w_in_ref.1) | copy-start | bytes 6291460
  3.6 0.7 copy-start.5
  114.8 1.4 %copy-start.1 = (bf16[2,512,1024]{2,1,0:T(8,128)(2,1)}, bf16[2,512,1024]{2,1,0:T(8,128)(2,1)S(1)}, u32[]{:S(2)}) copy-start(bf16[2,512,1024]{2,1,0:T(8,128)(2,1)S(1)} %get-tuple-element.17) | copy-start | bytes 6291460
  116.2 1.3 %copy-start.3 = (bf16[2,1024,512]{2,1,0:T(8,128)(2,1)}, bf16[2,1024,512]{2,1,0:T(8,128)(2,1)S(1)}, u32[]{:S(2)}) copy-start(bf16[2,1024,512]{2,1,0:T(8,128)(2,1)S(1)} %get-tuple-element.16) | copy-start | bytes 6291460
  117.5 1.8 %copy-start.4 = (bf16[2,1024,512]{2,1,0:T(8,128)(2,1)S(1)}, bf16[2,1024,512]{2,1,0:T(8,128)(2,1)}, u32[]{:S(2)}) copy-start(bf16[2,1024,512]{2,1,0:T(8,128)(2,1)} %copy-done.3) | copy-start | bytes 6291460
  119.3 2.3 %copy-start.2 = (bf16[2,512,1024]{2,1,0:T(8,128)(2,1)S(1)}, bf16[2,512,1024]{2,1,0:T(8,128)(2,1)}, u32[]{:S(2)}) copy-start(bf16[2,512,1024]{2,1,0:T(8,128)(2,1)} %copy-done.1) | copy-start | bytes 6291460

commit v3 on v2

--- a/solution.py
+++ b/solution.py
@@ -17,32 +17,46 @@
 DEPTH = 2
 TAIL = 4
 
+SEND, MLP, BACK, WEIGHTS, END = range(5)
+NAMES = [f"{kind}{k}" for kind in "scp" for k in range(4)] + ["o", "p"]
 ORDER = {
     0: [
-        "f.l.o.c0.1", "f.r.s0.s0.0", "f.l.p.c1.0", "f.r.c3.c3.1", "f.l.p.c1.1", "f.r.c2.c2.0", "f.r.c2.c2.1", "f.l.o.c0.0", "f.r.s0.s0.1", "m.2.1",
-        "b.r.s2.1", "m.3.0", "b.r.s3.0", "f.r.c3.c3.0", "m.0.1", "b.r.c0.1", "m.1.0", "b.r.c1.0", "b.r.s1.0", "m.1.1",
-        "b.r.s1.1", "b.r.c1.1", "m.0.0", "b.r.c0.0", "m.3.1", "b.r.s3.1", "m.2.0", "b.l.c2.0", "b.r.s2.0", "b.l.c2.1",
-        "b.r.p1.0", "b.l.c3.1", "b.l.c3.0", "b.r.p1.1", "w.0", "e.1", "e.0", "w.1", "w.2", "w.3",
+        (0, 0, 12, 4, 0), (0, 0, 12, 4, 1), (0, 1, 7, 7, 0), (0, 0, 13, 5, 0), (0, 1, 7, 7, 1), (0, 0, 13, 5, 1),
+        (0, 1, 6, 6, 0), (0, 1, 6, 6, 1), (0, 1, 0, 0, 0), (1, 2, 0), (2, 1, 2, 0), (0, 1, 0, 0, 1),
+        (1, 0, 0), (2, 1, 4, 0), (1, 0, 1), (2, 1, 4, 1), (1, 1, 0), (2, 1, 5, 0),
+        (2, 1, 1, 0), (1, 1, 1), (2, 1, 5, 1), (1, 2, 1), (2, 1, 2, 1), (2, 1, 1, 1),
+        (1, 3, 0), (2, 1, 3, 0), (1, 3, 1), (2, 1, 3, 1), (2, 0, 6, 0), (2, 0, 6, 1),
+        (2, 0, 7, 0), (2, 1, 9, 0), (2, 1, 9, 1), (2, 0, 7, 1), (4, 0), (3, 0),
+        (4, 1), (3, 1), (3, 2), (3, 3),
     ],
     1: [
-        "f.l.o.p.0", "f.l.o.p.1", "f.r.s1.s1.0", "f.l.s1.s1.1", "f.r.s1.s1.1", "f.l.s1.s1.0", "f.r.s0.s0.0", "f.r.c3.c3.1", "f.l.s2.s2.1", "m.2.0",
-        "f.l.s3.s3.0", "f.r.c2.c2.0", "f.l.c0.c0.1", "f.r.c2.c2.1", "m.1.0", "f.l.c1.c1.0", "f.r.s0.s0.1", "m.1.1", "f.l.c1.c1.1", "f.r.c3.c3.0",
-        "f.l.s3.s3.1", "b.r.c1.0", "f.l.c0.c0.0", "m.3.0", "b.r.s3.0", "m.0.0", "f.l.s2.s2.0", "m.0.1", "b.r.c0.1", "b.r.c1.1",
-        "b.l.c2.0", "m.2.1", "b.r.s2.1", "b.l.c2.1", "b.r.c0.0", "m.3.1", "b.l.c3.1", "w.0", "b.r.s3.1", "w.1",
-        "b.l.c3.0", "b.r.s2.0", "b.l.s0.1", "w.2", "w.3", "b.l.s0.0", "e.0", "e.1",
+        (0, 0, 12, 13, 0), (0, 0, 12, 13, 1), (0, 1, 1, 1, 0), (0, 1, 1, 1, 1), (0, 0, 1, 1, 1), (0, 0, 2, 2, 0),
+        (0, 1, 7, 7, 0), (0, 1, 7, 7, 1), (0, 0, 1, 1, 0), (0, 0, 4, 4, 0), (0, 1, 6, 6, 0), (1, 2, 0),
+        (0, 0, 4, 4, 1), (0, 1, 6, 6, 1), (0, 0, 5, 5, 0), (1, 1, 0), (0, 0, 5, 5, 1), (2, 1, 2, 0),
+        (0, 1, 0, 0, 0), (1, 1, 1), (1, 0, 1), (0, 1, 0, 0, 1), (0, 0, 2, 2, 1), (2, 1, 4, 1),
+        (0, 0, 3, 3, 0), (2, 1, 5, 0), (0, 0, 3, 3, 1), (2, 1, 5, 1), (1, 3, 0), (1, 0, 0),
+        (2, 1, 4, 0), (2, 0, 6, 0), (1, 2, 1), (2, 0, 6, 1), (2, 1, 2, 1), (2, 0, 7, 0),
+        (2, 1, 3, 0), (1, 3, 1), (2, 0, 7, 1), (2, 1, 3, 1), (2, 0, 0, 0), (3, 0),
+        (3, 1), (2, 0, 0, 1), (4, 0), (4, 1), (3, 2), (3, 3),
     ],
     2: [
-        "f.r.o.p.0", "f.r.o.p.1", "f.l.s2.s2.0", "f.r.s2.s2.1", "f.l.s2.s2.1", "f.r.s2.s2.0", "f.l.s3.s3.0", "f.l.c0.c0.1", "f.r.s1.s1.1", "m.1.0",
-        "f.r.s0.s0.0", "f.l.c1.c1.0", "f.r.c3.c3.1", "f.l.c1.c1.1", "m.2.0", "f.r.c2.c2.0", "f.l.s3.s3.1", "m.2.1", "f.r.c2.c2.1", "f.l.c0.c0.0",
-        "f.r.s0.s0.1", "b.l.c2.0", "f.r.c3.c3.0", "m.0.0", "b.l.s0.0", "m.3.0", "f.r.s1.s1.0", "m.3.1", "b.l.c3.1", "b.l.c2.1",
-        "b.r.c1.0", "m.1.1", "b.l.s1.1", "b.r.c1.1", "b.l.c3.0", "m.0.1", "b.r.c0.1", "w.0", "b.l.s0.1", "w.1",
-        "b.r.c0.0", "b.l.s1.0", "b.r.s3.1", "w.2", "w.3", "b.r.s3.0", "e.0", "e.1",
+        (0, 1, 12, 13, 0), (0, 1, 12, 13, 1), (0, 0, 2, 2, 0), (0, 0, 2, 2, 1), (0, 1, 2, 2, 1), (0, 1, 1, 1, 0),
+        (0, 0, 4, 4, 0), (0, 0, 4, 4, 1), (0, 1, 2, 2, 0), (0, 1, 7, 7, 0), (0, 0, 5, 5, 0), (1, 1, 0),
+        (0, 1, 7, 7, 1), (0, 0, 5, 5, 1), (0, 1, 6, 6, 0), (1, 2, 0), (0, 1, 6, 6, 1), (2, 0, 1, 0),
+        (0, 0, 3, 3, 0), (1, 2, 1), (1, 3, 1), (0, 0, 3, 3, 1), (0, 1, 1, 1, 1), (2, 0, 7, 1),
+        (0, 1, 0, 0, 0), (2, 0, 6, 0), (0, 1, 0, 0, 1), (2, 0, 6, 1), (1, 0, 0), (1, 3, 0),
+        (2, 0, 7, 0), (2, 1, 5, 0), (1, 1, 1), (2, 1, 5, 1), (2, 0, 1, 1), (2, 1, 4, 0),
+        (2, 0, 0, 0), (1, 0, 1), (2, 1, 4, 1), (2, 0, 0, 1), (2, 1, 3, 0), (3, 0),
+        (3, 1), (2, 1, 3, 1), (4, 0), (4, 1), (3, 2), (3, 3),
     ],
     3: [
-        "f.r.o.c3.1", "f.l.s3.s3.0", "f.r.p.c2.0", "f.l.c0.c0.1", "f.r.p.c2.1", "f.l.c1.c1.0", "f.l.c1.c1.1", "f.r.o.c3.0", "f.l.s3.s3.1", "m.1.1",
-        "b.l.s1.1", "m.0.0", "b.l.s0.0", "f.l.c0.c0.0", "m.3.1", "b.l.c3.1", "m.2.0", "b.l.c2.0", "b.l.s2.0", "m.2.1",
-        "b.l.s2.1", "b.l.c2.1", "m.3.0", "b.l.c3.0", "m.0.1", "b.l.s0.1", "m.1.0", "b.r.c1.0", "b.l.s1.0", "b.r.c1.1",
-        "b.l.p2.0", "b.r.c0.1", "b.r.c0.0", "b.l.p2.1", "w.0", "e.1", "e.0", "w.1", "w.2", "w.3",
+        (0, 1, 12, 7, 0), (0, 1, 12, 7, 1), (0, 0, 4, 4, 0), (0, 1, 13, 6, 0), (0, 0, 4, 4, 1), (0, 1, 13, 6, 1),
+        (0, 0, 5, 5, 0), (0, 0, 5, 5, 1), (0, 0, 3, 3, 0), (1, 1, 0), (2, 0, 1, 0), (0, 0, 3, 3, 1),
+        (1, 3, 0), (2, 0, 7, 0), (1, 3, 1), (2, 0, 7, 1), (1, 2, 0), (2, 0, 6, 0),
+        (2, 0, 2, 0), (1, 2, 1), (2, 0, 6, 1), (1, 1, 1), (2, 0, 1, 1), (2, 0, 2, 1),
+        (1, 0, 0), (2, 0, 0, 0), (1, 0, 1), (2, 0, 0, 1), (2, 1, 5, 0), (2, 1, 5, 1),
+        (2, 1, 4, 0), (2, 0, 10, 0), (2, 0, 10, 1), (2, 1, 4, 1), (4, 0), (3, 0),
+        (4, 1), (3, 1), (3, 2), (3, 3),
     ],
 }
 
@@ -84,29 +98,30 @@
         if (name, head) not in here:
             here.add((name, head))
             kind = {"o": "out", f"s{case}": "own"}.get(name, "arrived")
-            now.append((kind, name, int(head)))
-
-    for item in ORDER[case]:
-        item = item.split(".")
-        if item[0] in "mw":
-            if item[0] == "m":
-                mlps.append((int(item[1]), int(item[2])))
-                arrive("s" + item[1], item[2])
-                arrive("c" + item[1], item[2])
+            now.append((kind, name, head))
+
+    for kind, *item in ORDER[case]:
+        if kind in (MLP, WEIGHTS):
+            if kind == MLP:
+                mlps.append(tuple(item))
+                arrive(f"s{item[0]}", item[1])
+                arrive(f"c{item[0]}", item[1])
             parts.append(now)
             now = []
             continue
-        if item[0] == "e":
-            now.append(("end", int(item[1])))
+        if kind == END:
+            now.append(("end", item[0]))
             continue
-        if item[0] == "f":
-            arrive(item[2], item[-1])
-        turns = sent[item[1]]
+        way, head = "lr"[item[0]], item[-1]
+        names = [NAMES[at] for at in item[1:-1]]
+        if kind == SEND:
+            arrive(names[0], head)
+        turns = sent[way]
         late = len(turns) - DEPTH
         if late >= 0:
-            now.append(("sent", turns[late], item[1], late))
-        now.append((item[0], *item[1:-1], int(item[-1]), len(turns)))
-        turns.append(item[0])
+            now.append(("sent", turns[late], way, late))
+        turns.append("f" if kind == SEND else "b")
+        now.append((turns[-1], way, *names, head, len(turns) - 1))
         if len(sent["l"]) + len(sent["r"]) == 3:
             now.append(("prepare",))
     parts.append(now)
@@ -116,8 +131,8 @@
 
 
 def kernel(
-    input_ref, cotangent_ref, gain_ref, w_in_ref, w_out_ref, returned_ref, grad_in, grad_out,
-    parts, gain, slots, sums, from_left, from_right, final, got, w_in, w_in_t, w_out, normed, cotangent, act, pre_grad,
+    input_ref, cotangent_ref, gains_ref, w_in_ref, w_out_ref, returned_ref, grad_in, grad_out,
+    parts, gains, gain, slots, sums, from_left, from_right, final, got, w_in, w_in_t, w_out, normed, cotangent, act, pre_grad,
     plane_send, plane_recv, ring_send, ring_recv, left_recv, right_recv, back_send, back_recv, weight_sem,
 ):
     here = place()
@@ -126,8 +141,10 @@
     own = half * 4 + zl
     load_in = pltpu.make_async_copy(w_in_ref, w_in, weight_sem.at[0])
     load_out = pltpu.make_async_copy(w_out_ref, w_out, weight_sem.at[1])
+    load_gain = pltpu.make_async_copy(gains_ref, gains, weight_sem.at[2])
     load_in.start()
     load_out.start()
+    load_gain.start()
 
     barrier = pltpu.get_barrier_semaphore()
 
@@ -170,6 +187,7 @@
     def prepare():
         load_in.wait()
         load_out.wait()
+        load_gain.wait()
 
         def turn(at, carry):
             token, chunk = at // 4, lax.rem(at, 4)
@@ -179,7 +197,7 @@
 
         lax.fori_loop(0, 8, turn, 0)
         for token in range(2):
-            wide = jnp.broadcast_to(gain_ref[token : token + 1, :], (128, WIDTH)).T
+            wide = jnp.broadcast_to(gains[token : token + 1, :], (128, WIDTH)).T
             gain[token] = wide.reshape(COLUMNS, 2, 32, 128)
 
     targets = {"l": z_neighbour(*here, -1), "r": z_neighbour(*here, 1)}
@@ -359,6 +377,18 @@
         wait_for(got.at[head, pl.ds(0, PEERS - 1)], back_send.at[head])
 
 
+def store(returned, turned, grad_in, grad_out, total, grad_in_out, grad_out_out, sems):
+    copies = []
+    for which, (ref, to) in enumerate(((grad_in, grad_in_out), (grad_out, grad_out_out))):
+        for token in range(2):
+            copies.append(pltpu.make_async_copy(ref.at[token], to.at[token], sems.at[which, token]))
+    for copy in copies:
+        copy.start()
+    total[...] = (returned[...].astype(jnp.float32) + turned[...].astype(jnp.float32)).astype(jnp.bfloat16)
+    for copy in copies:
+        copy.wait()
+
+
 def per_device(block_input, out_grad, norm_gain, w_in, w_out):
     own_rows, local_tok, width = block_input.shape
     rows = local_tok * HEAD
@@ -376,10 +406,11 @@
             jax.ShapeDtypeStruct(w_in.shape, bf16),
             jax.ShapeDtypeStruct(w_out.shape, bf16),
         ),
-        in_specs=[inside, inside, inside, anywhere, anywhere],
+        in_specs=[inside, inside, anywhere, anywhere, anywhere],
         out_specs=(inside, inside, inside),
         scratch_shapes=[
             pltpu.VMEM((2, 2, COLUMNS, 2, 2, rows, own_rows), bf16),
+            pltpu.VMEM((2, width), jnp.float32),
             pltpu.VMEM((2, COLUMNS, 2, 2 * rows, own_rows), jnp.float32),
             pltpu.VMEM((PLANES + 2, 2, 2, *block), bf16),
             pltpu.VMEM((PLANES, 2, *block), bf16),
@@ -402,15 +433,25 @@
             dma((PLANES + 1, 2)),
             dma((2,)),
             dma((2,)),
-            dma((2,)),
+            dma((3,)),
         ],
         compiler_params=pltpu.CompilerParams(
-            collective_id=0, has_side_effects=True, vmem_limit_bytes=46 * 2**20
+            collective_id=0, has_side_effects=True, vmem_limit_bytes=47 * 2**20
         ),
     )(block_input.transpose(1, 2, 0), turned, norm_gain, w_in, w_out)
-    returned = returned.reshape(local_tok, width, own_rows)
-    input_grad = (turned.astype(jnp.float32) + returned.astype(jnp.float32)).astype(jnp.bfloat16)
-    return (input_grad.transpose(2, 0, 1), grad_in, grad_out)
+    total, grad_in, grad_out = pl.pallas_call(
+        store,
+        out_shape=(
+            jax.ShapeDtypeStruct(turned.shape, bf16),
+            jax.ShapeDtypeStruct(w_in.shape, bf16),
+            jax.ShapeDtypeStruct(w_out.shape, bf16),
+        ),
+        in_specs=[inside, inside, inside, inside],
+        out_specs=(inside, anywhere, anywhere),
+        scratch_shapes=[dma((2, 2))],
+        compiler_params=pltpu.CompilerParams(vmem_limit_bytes=2**23),
+    )(returned.reshape(turned.shape), turned, grad_in, grad_out)
+    return (total.transpose(2, 0, 1), grad_in, grad_out)
 
 
 def solution(mesh):

time: 123 us -> 117 us (0.951)
  local copies, waits for them, and re-layouts: 11.5 us -> 3.88 us
    unnamed x17 -> x5, local copies, waits for them, and re-layouts: 11.5 us -> 3.88 us
    pallas_call x0 -> x1, Pallas kernels: none -> 2.04 us  [per_device(): pl.pallas_call(store, out_shape=(jax.ShapeDtypeStruct(turned.shape, bf16)...]
where the time goes in v3:
time: 117 us
  Pallas kernels  112 us (96%)
  local copies, waits for them, and re-layouts  3.88 us (3%)
    pallas_call x1, Pallas kernels, per_device(): pl.pallas_call(kernel, out_shape=(jax.ShapeDtypeStruct((local_tok, COLUMN...  110 us
    unnamed x5, local copies, waits for them, and re-layouts  3.88 us

profile of v3, /device:TPU:1, one launch (start us, length us, event | category | flops | bytes accessed | tf_op | source)
XLA Modules:
  0.0 116.9 jit_solution(3421929548970718790)
XLA Ops:
  0.6 0.0 copy-start
  0.6 1.4 %copy.8 = bf16[128,2,1024]{0,2,1:T(8,128)(2,1)S(1)} copy(bf16[128,2,1024]{2,1,0:T(2,128)(2,1)} %param.5) | data formatting | bytes 1048576 | tf_op args[0]
  2.0 1.4 %copy.9 = bf16[128,2,1024]{0,2,1:T(8,128)(2,1)S(1)} copy(bf16[128,2,1024]{2,1,0:T(2,128)(2,1)} %param.6) | data formatting | bytes 1048576 | tf_op args[1]
  3.4 0.0 copy-done
  3.4 110.3 %shard_map.76 = (bf16[2,16,2,2,16,128]{5,4,3,2,1,0:T(8,128)(2,1)S(1)}, bf16[2,1024,512]{2,1,0:T(8,128)(2,1)S(1)}, bf16[2,512,1024]{2,1,0:T(8,128)(2,1)S(1)}) custom-call(bf16[2,1024,128]{2,1,0:T(8,128)(2,1)S(1)} %bitcast.6, bf16[2,1024,128]{2,1,0:T(8,128)(2,1)S(1)} %bitcast.4, f32[2,1024]{1,0:T(2,128)S(1)} %copy-done, bf16[2,1024,512]{2,1,0:T(8,128)(2,1)} %w_in_ref.1, ...), custom_call_target="tpu_custom_call" | custom-call | tf_op jit(solution)/shard_map/pallas_call | solution.py:402
  113.8 2.0 %shard_map.77 = (bf16[2,1024,128]{2,1,0:T(8,128)(2,1)S(1)}, bf16[2,1024,512]{2,1,0:T(8,128)(2,1)}, bf16[2,512,1024]{2,1,0:T(8,128)(2,1)}) custom-call(bf16[2,1024,128]{2,1,0:T(8,128)(2,1)S(1)} %bitcast.7, bf16[2,1024,128]{2,1,0:T(8,128)(2,1)S(1)} %bitcast.5, bf16[2,1024,512]{2,1,0:T(8,128)(2,1)S(1)} %get-tuple-element.10.grad_in, ...), custom_call_target="tpu_custom_call" | custom-call | tf_op jit(solution)/shard_map/pallas_call | solution.py:442
  115.8 1.1 copy.10
Async XLA Ops:
  0.6 2.8 %copy-start = (f32[2,1024]{1,0:T(2,128)S(1)}, f32[2,1024]{1,0:T(2,128)}, u32[]{:S(2)}) copy-start(f32[2,1024]{1,0:T(2,128)} %gains_ref.1) | copy-start | bytes 24580

commit v4 on v3

--- a/solution.py
+++ b/solution.py
@@ -21,42 +21,42 @@
 NAMES = [f"{kind}{k}" for kind in "scp" for k in range(4)] + ["o", "p"]
 ORDER = {
     0: [
-        (0, 0, 12, 4, 0), (0, 0, 12, 4, 1), (0, 1, 7, 7, 0), (0, 0, 13, 5, 0), (0, 1, 7, 7, 1), (0, 0, 13, 5, 1),
-        (0, 1, 6, 6, 0), (0, 1, 6, 6, 1), (0, 1, 0, 0, 0), (1, 2, 0), (2, 1, 2, 0), (0, 1, 0, 0, 1),
-        (1, 0, 0), (2, 1, 4, 0), (1, 0, 1), (2, 1, 4, 1), (1, 1, 0), (2, 1, 5, 0),
-        (2, 1, 1, 0), (1, 1, 1), (2, 1, 5, 1), (1, 2, 1), (2, 1, 2, 1), (2, 1, 1, 1),
-        (1, 3, 0), (2, 1, 3, 0), (1, 3, 1), (2, 1, 3, 1), (2, 0, 6, 0), (2, 0, 6, 1),
-        (2, 0, 7, 0), (2, 1, 9, 0), (2, 1, 9, 1), (2, 0, 7, 1), (4, 0), (3, 0),
-        (4, 1), (3, 1), (3, 2), (3, 3),
+        (0, 0, 12, 4, 0), (0, 0, 12, 4, 1), (0, 0, 13, 5, 0), (0, 1, 7, 7, 0), (0, 1, 7, 7, 1), (0, 0, 13, 5, 1),
+        (0, 1, 6, 6, 0), (0, 1, 6, 6, 1), (1, 2, 0), (0, 1, 0, 0, 0), (0, 1, 0, 0, 1), (1, 0, 0),
+        (2, 1, 4, 0), (1, 0, 1), (2, 1, 4, 1), (2, 1, 2, 0), (1, 1, 0), (2, 1, 5, 0),
+        (2, 1, 1, 0), (1, 1, 1), (2, 1, 5, 1), (2, 1, 1, 1), (1, 3, 0), (2, 1, 3, 0),
+        (1, 3, 1), (2, 1, 3, 1), (2, 0, 6, 0), (1, 2, 1), (2, 1, 2, 1), (2, 0, 6, 1),
+        (3, 0), (2, 0, 7, 1), (2, 1, 9, 0), (2, 0, 7, 0), (2, 1, 9, 1), (4, 1),
+        (4, 0), (3, 1), (3, 2), (3, 3),
     ],
     1: [
         (0, 0, 12, 13, 0), (0, 0, 12, 13, 1), (0, 1, 1, 1, 0), (0, 1, 1, 1, 1), (0, 0, 1, 1, 1), (0, 0, 2, 2, 0),
-        (0, 1, 7, 7, 0), (0, 1, 7, 7, 1), (0, 0, 1, 1, 0), (0, 0, 4, 4, 0), (0, 1, 6, 6, 0), (1, 2, 0),
-        (0, 0, 4, 4, 1), (0, 1, 6, 6, 1), (0, 0, 5, 5, 0), (1, 1, 0), (0, 0, 5, 5, 1), (2, 1, 2, 0),
-        (0, 1, 0, 0, 0), (1, 1, 1), (1, 0, 1), (0, 1, 0, 0, 1), (0, 0, 2, 2, 1), (2, 1, 4, 1),
-        (0, 0, 3, 3, 0), (2, 1, 5, 0), (0, 0, 3, 3, 1), (2, 1, 5, 1), (1, 3, 0), (1, 0, 0),
-        (2, 1, 4, 0), (2, 0, 6, 0), (1, 2, 1), (2, 0, 6, 1), (2, 1, 2, 1), (2, 0, 7, 0),
-        (2, 1, 3, 0), (1, 3, 1), (2, 0, 7, 1), (2, 1, 3, 1), (2, 0, 0, 0), (3, 0),
-        (3, 1), (2, 0, 0, 1), (4, 0), (4, 1), (3, 2), (3, 3),
+        (0, 1, 7, 7, 0), (0, 0, 1, 1, 0), (0, 1, 7, 7, 1), (0, 0, 4, 4, 0), (0, 1, 6, 6, 0), (1, 2, 0),
+        (0, 0, 4, 4, 1), (0, 1, 6, 6, 1), (1, 2, 1), (0, 0, 5, 5, 0), (0, 1, 0, 0, 0), (1, 0, 0),
+        (0, 0, 5, 5, 1), (0, 1, 0, 0, 1), (1, 1, 0), (0, 0, 3, 3, 0), (2, 1, 4, 0), (0, 0, 3, 3, 1),
+        (2, 1, 2, 0), (1, 3, 1), (2, 1, 5, 0), (1, 0, 1), (2, 1, 4, 1), (0, 0, 2, 2, 1),
+        (1, 1, 1), (2, 1, 5, 1), (2, 0, 6, 0), (2, 0, 6, 1), (2, 0, 7, 1), (2, 1, 3, 1),
+        (1, 3, 0), (2, 0, 7, 0), (2, 1, 3, 0), (3, 0), (3, 1), (2, 0, 0, 1),
+        (2, 0, 0, 0), (2, 1, 2, 1), (3, 2), (4, 0), (4, 1), (3, 3),
     ],
     2: [
         (0, 1, 12, 13, 0), (0, 1, 12, 13, 1), (0, 0, 2, 2, 0), (0, 0, 2, 2, 1), (0, 1, 2, 2, 1), (0, 1, 1, 1, 0),
-        (0, 0, 4, 4, 0), (0, 0, 4, 4, 1), (0, 1, 2, 2, 0), (0, 1, 7, 7, 0), (0, 0, 5, 5, 0), (1, 1, 0),
-        (0, 1, 7, 7, 1), (0, 0, 5, 5, 1), (0, 1, 6, 6, 0), (1, 2, 0), (0, 1, 6, 6, 1), (2, 0, 1, 0),
-        (0, 0, 3, 3, 0), (1, 2, 1), (1, 3, 1), (0, 0, 3, 3, 1), (0, 1, 1, 1, 1), (2, 0, 7, 1),
-        (0, 1, 0, 0, 0), (2, 0, 6, 0), (0, 1, 0, 0, 1), (2, 0, 6, 1), (1, 0, 0), (1, 3, 0),
-        (2, 0, 7, 0), (2, 1, 5, 0), (1, 1, 1), (2, 1, 5, 1), (2, 0, 1, 1), (2, 1, 4, 0),
-        (2, 0, 0, 0), (1, 0, 1), (2, 1, 4, 1), (2, 0, 0, 1), (2, 1, 3, 0), (3, 0),
-        (3, 1), (2, 1, 3, 1), (4, 0), (4, 1), (3, 2), (3, 3),
+        (0, 0, 4, 4, 0), (0, 1, 2, 2, 0), (0, 0, 4, 4, 1), (0, 1, 7, 7, 0), (0, 0, 5, 5, 0), (1, 1, 0),
+        (0, 1, 7, 7, 1), (0, 0, 5, 5, 1), (1, 1, 1), (0, 1, 6, 6, 0), (0, 0, 3, 3, 0), (1, 3, 0),
+        (0, 1, 6, 6, 1), (0, 0, 3, 3, 1), (1, 2, 0), (0, 1, 0, 0, 0), (2, 0, 7, 0), (0, 1, 0, 0, 1),
+        (2, 0, 1, 0), (1, 0, 1), (2, 0, 6, 0), (1, 3, 1), (2, 0, 7, 1), (0, 1, 1, 1, 1),
+        (1, 2, 1), (2, 0, 6, 1), (2, 1, 5, 0), (2, 1, 5, 1), (2, 1, 4, 1), (2, 0, 0, 1),
+        (1, 0, 0), (2, 1, 4, 0), (2, 0, 0, 0), (3, 0), (3, 1), (2, 1, 3, 1),
+        (2, 1, 3, 0), (2, 0, 1, 1), (3, 2), (4, 0), (4, 1), (3, 3),
     ],
     3: [
-        (0, 1, 12, 7, 0), (0, 1, 12, 7, 1), (0, 0, 4, 4, 0), (0, 1, 13, 6, 0), (0, 0, 4, 4, 1), (0, 1, 13, 6, 1),
-        (0, 0, 5, 5, 0), (0, 0, 5, 5, 1), (0, 0, 3, 3, 0), (1, 1, 0), (2, 0, 1, 0), (0, 0, 3, 3, 1),
-        (1, 3, 0), (2, 0, 7, 0), (1, 3, 1), (2, 0, 7, 1), (1, 2, 0), (2, 0, 6, 0),
-        (2, 0, 2, 0), (1, 2, 1), (2, 0, 6, 1), (1, 1, 1), (2, 0, 1, 1), (2, 0, 2, 1),
-        (1, 0, 0), (2, 0, 0, 0), (1, 0, 1), (2, 0, 0, 1), (2, 1, 5, 0), (2, 1, 5, 1),
-        (2, 1, 4, 0), (2, 0, 10, 0), (2, 0, 10, 1), (2, 1, 4, 1), (4, 0), (3, 0),
-        (4, 1), (3, 1), (3, 2), (3, 3),
+        (0, 1, 12, 7, 0), (0, 1, 12, 7, 1), (0, 1, 13, 6, 0), (0, 0, 4, 4, 0), (0, 0, 4, 4, 1), (0, 1, 13, 6, 1),
+        (0, 0, 5, 5, 0), (0, 0, 5, 5, 1), (1, 1, 0), (0, 0, 3, 3, 0), (0, 0, 3, 3, 1), (1, 3, 0),
+        (2, 0, 7, 0), (1, 3, 1), (2, 0, 7, 1), (2, 0, 1, 0), (1, 2, 0), (2, 0, 6, 0),
+        (2, 0, 2, 0), (1, 2, 1), (2, 0, 6, 1), (2, 0, 2, 1), (1, 0, 0), (2, 0, 0, 0),
+        (1, 0, 1), (2, 0, 0, 1), (2, 1, 5, 0), (1, 1, 1), (2, 0, 1, 1), (2, 1, 5, 1),
+        (3, 0), (2, 1, 4, 1), (2, 0, 10, 0), (2, 1, 4, 0), (2, 0, 10, 1), (4, 1),
+        (4, 0), (3, 1), (3, 2), (3, 3),
     ],
 }
 
@@ -158,7 +158,8 @@
         pl.semaphore_signal(barrier, inc=1, device_id=z_neighbour(*here, step), device_id_type=MESH)
 
     for which, ref in enumerate((input_ref, cotangent_ref)):
-        tokens = [ref[token].astype(jnp.float32).reshape(COLUMNS, 2, 2, 2, HEAD, 128) for token in range(2)]
+        whole = ref[...].astype(jnp.float32)
+        tokens = [whole[:, token, :].T.reshape(COLUMNS, 2, 2, 2, HEAD, 128) for token in range(2)]
         for to_half, to_core, head in ((a, b, c) for a in range(2) for b in range(2) for c in range(2)):
             both = jnp.stack([token[:, to_half, to_core, head] for token in tokens], axis=1)
             parts[to_half, head, :, to_core, which] = both.reshape(COLUMNS, 2 * HEAD, 128).astype(jnp.bfloat16)
@@ -377,14 +378,15 @@
         wait_for(got.at[head, pl.ds(0, PEERS - 1)], back_send.at[head])
 
 
-def store(returned, turned, grad_in, grad_out, total, grad_in_out, grad_out_out, sems):
+def store(returned, out_grad, grad_in, grad_out, total, grad_in_out, grad_out_out, sems):
     copies = []
     for which, (ref, to) in enumerate(((grad_in, grad_in_out), (grad_out, grad_out_out))):
         for token in range(2):
             copies.append(pltpu.make_async_copy(ref.at[token], to.at[token], sems.at[which, token]))
     for copy in copies:
         copy.start()
-    total[...] = (returned[...].astype(jnp.float32) + turned[...].astype(jnp.float32)).astype(jnp.bfloat16)
+    both = jnp.stack([returned[token].astype(jnp.float32).T for token in range(2)], axis=1)
+    total[...] = (both + out_grad[...].astype(jnp.float32)).astype(jnp.bfloat16)
     for copy in copies:
         copy.wait()
 
@@ -398,7 +400,6 @@
     anywhere = pl.BlockSpec(memory_space=pl.ANY)
     inside = pl.BlockSpec(memory_space=pltpu.VMEM)
     dma = pltpu.SemaphoreType.DMA
-    turned = out_grad.transpose(1, 2, 0)
     returned, grad_in, grad_out = pl.pallas_call(
         kernel,
         out_shape=(
@@ -438,11 +439,11 @@
         compiler_params=pltpu.CompilerParams(
             collective_id=0, has_side_effects=True, vmem_limit_bytes=47 * 2**20
         ),
-    )(block_input.transpose(1, 2, 0), turned, norm_gain, w_in, w_out)
+    )(block_input, out_grad, norm_gain, w_in, w_out)
     total, grad_in, grad_out = pl.pallas_call(
         store,
         out_shape=(
-            jax.ShapeDtypeStruct(turned.shape, bf16),
+            jax.ShapeDtypeStruct(out_grad.shape, bf16),
             jax.ShapeDtypeStruct(w_in.shape, bf16),
             jax.ShapeDtypeStruct(w_out.shape, bf16),
         ),
@@ -450,8 +451,8 @@
         out_specs=(inside, anywhere, anywhere),
         scratch_shapes=[dma((2, 2))],
         compiler_params=pltpu.CompilerParams(vmem_limit_bytes=2**23),
-    )(returned.reshape(turned.shape), turned, grad_in, grad_out)
-    return (total.transpose(2, 0, 1), grad_in, grad_out)
+    )(returned.reshape(local_tok, width, own_rows), out_grad, grad_in, grad_out)
+    return (total, grad_in, grad_out)
 
 
 def solution(mesh):

time: 117 us -> 117 us (level)
    unnamed x5 -> x6, local copies, waits for them, and re-layouts: 3.88 us -> 2.77 us
where the time goes in v4:
time: 117 us; the launch traced here: 116 us
  Pallas kernels  113 us (97%)
  local copies, waits for them, and re-layouts  2.77 us (2%)
    pallas_call x1, Pallas kernels, per_device(): pl.pallas_call(kernel, out_shape=(jax.ShapeDtypeStruct((local_tok, COLUMN...  110 us
    pallas_call x1, Pallas kernels, per_device(): pl.pallas_call(store, out_shape=(jax.ShapeDtypeStruct(out_grad.shape, bf1...  2.85 us
    unnamed x6, local copies, waits for them, and re-layouts  2.77 us

profile of v4, /device:TPU:1, one launch (start us, length us, event | category | flops | bytes accessed | tf_op | source)
XLA Modules:
  0.0 116.3 jit_solution(18137325087021591530)
XLA Ops:
  0.6 0.0 copy-start
  0.6 1.0 copy-done
  1.7 0.0 copy-start.1
  1.7 1.0 copy-done.1
  2.7 0.0 copy-start.2
  2.7 0.7 copy-done.2
  3.4 110.0 %shard_map.76 = (bf16[2,16,2,2,16,128]{5,4,3,2,1,0:T(8,128)(2,1)S(1)}, bf16[2,1024,512]{2,1,0:T(8,128)(2,1)S(1)}, bf16[2,512,1024]{2,1,0:T(8,128)(2,1)S(1)}) custom-call(bf16[128,2,1024]{2,1,0:T(2,128)(2,1)S(1)} %copy-done.1, bf16[128,2,1024]{2,1,0:T(2,128)(2,1)S(1)} %copy-done, f32[2,1024]{1,0:T(2,128)S(1)} %copy-done.2, bf16[2,1024,512]{2,1,0:T(8,128)(2,1)} %w_in_ref.1, ...), custom_call_target="tpu_custom_call" | custom-call | tf_op jit(solution)/shard_map/pallas_call | solution.py:403
  113.4 2.8 %shard_map.77 = (bf16[128,2,1024]{2,1,0:T(2,128)(2,1)}, bf16[2,1024,512]{2,1,0:T(8,128)(2,1)}, bf16[2,512,1024]{2,1,0:T(8,128)(2,1)}) custom-call(bf16[2,1024,128]{2,1,0:T(8,128)(2,1)S(1)} %bitcast.1, bf16[128,2,1024]{2,1,0:T(2,128)(2,1)S(1)} %copy-done, bf16[2,1024,512]{2,1,0:T(8,128)(2,1)S(1)} %get-tuple-element.7.grad_in, ...), custom_call_target="tpu_custom_call" | custom-call | tf_op jit(solution)/shard_map/pallas_call | solution.py:443
Async XLA Ops:
  0.6 1.0 copy-start
  1.7 1.0 copy-start.1
  2.7 0.7 copy-start.2

commit v5 on v4

--- a/solution.py
+++ b/solution.py
@@ -15,6 +15,7 @@
 PLANES = 8
 OUT, PASS = 8, 9
 DEPTH = 2
+EARLY = 1
 TAIL = 4
 
 SEND, MLP, BACK, WEIGHTS, END = range(5)
@@ -122,6 +123,8 @@
             now.append(("sent", turns[late], way, late))
         turns.append("f" if kind == SEND else "b")
         now.append((turns[-1], way, *names, head, len(turns) - 1))
+        if len(sent["l"]) + len(sent["r"]) == 1:
+            now += [("exchange", which) for which in range(EARLY, 4)]
         if len(sent["l"]) + len(sent["r"]) == 3:
             now.append(("prepare",))
     parts.append(now)
@@ -166,9 +169,11 @@
     pl.semaphore_wait(barrier, PEERS + 1)
 
     phases = [(1 - half, OUT, 0), (1 - half, OUT, 1), (half, own, 0), (half, own, 1)]
-    for which, (part, slot, head) in enumerate(phases):
-
-        def send(ahead, carry, which=which, part=part, slot=slot, head=head):
+
+    def exchange(which):
+        part, slot, head = phases[which]
+
+        def send(ahead, carry):
             peer, target = plane_peer(*here, ahead)
             pltpu.make_async_remote_copy(
                 src_ref=parts.at[part, head, peer // 2, lax.rem(peer, 2)],
@@ -184,6 +189,9 @@
         pltpu.make_async_copy(
             parts.at[part, head, column, core], slots.at[slot, head, :, me], plane_recv.at[which]
         ).start()
+
+    for which in range(EARLY):
+        exchange(which)
 
     def prepare():
         load_in.wait()
@@ -243,6 +251,9 @@
 
     def run(case, ops):
         for op in ops:
+            if op[0] == "exchange":
+                exchange(op[1])
+                continue
             if op[0] == "prepare":
                 prepare()
                 continue
@@ -385,8 +396,10 @@
             copies.append(pltpu.make_async_copy(ref.at[token], to.at[token], sems.at[which, token]))
     for copy in copies:
         copy.start()
-    both = jnp.stack([returned[token].astype(jnp.float32).T for token in range(2)], axis=1)
-    total[...] = (both + out_grad[...].astype(jnp.float32)).astype(jnp.bfloat16)
+    for rows in range(0, WIDTH, 256):
+        columns = slice(rows, rows + 256)
+        both = jnp.stack([returned[token, columns].T.astype(jnp.float32) for token in range(2)], axis=1)
+        total[:, :, columns] = (both + out_grad[:, :, columns].astype(jnp.float32)).astype(jnp.bfloat16)
     for copy in copies:
         copy.wait()
 

time: 117 us -> 116 us (level)
  no operation moved by 1% of the time
where the time goes in v5:
time: 116 us
  Pallas kernels  113 us (97%)
  local copies, waits for them, and re-layouts  2.77 us (2%)
    pallas_call x1, Pallas kernels, per_device(): pl.pallas_call(kernel, out_shape=(jax.ShapeDtypeStruct((local_tok, COLUMN...  110 us
    pallas_call x1, Pallas kernels, per_device(): pl.pallas_call(store, out_shape=(jax.ShapeDtypeStruct(out_grad.shape, bf1...  2.89 us
    unnamed x6, local copies, waits for them, and re-layouts  2.77 us

profile of v5, /device:TPU:1, one launch (start us, length us, event | category | flops | bytes accessed | tf_op | source)
XLA Modules:
  0.0 116.2 jit_solution(14073439138550961290)
XLA Ops:
  0.6 0.0 copy-start
  0.6 1.0 copy-done
  1.7 0.0 copy-start.1
  1.7 1.0 copy-done.1
  2.7 0.0 copy-start.2
  2.7 0.7 copy-done.2
  3.4 109.9 %shard_map.76 = (bf16[2,16,2,2,16,128]{5,4,3,2,1,0:T(8,128)(2,1)S(1)}, bf16[2,1024,512]{2,1,0:T(8,128)(2,1)S(1)}, bf16[2,512,1024]{2,1,0:T(8,128)(2,1)S(1)}) custom-call(bf16[128,2,1024]{2,1,0:T(2,128)(2,1)S(1)} %copy-done.1, bf16[128,2,1024]{2,1,0:T(2,128)(2,1)S(1)} %copy-done, f32[2,1024]{1,0:T(2,128)S(1)} %copy-done.2, bf16[2,1024,512]{2,1,0:T(8,128)(2,1)} %w_in_ref.1, ...), custom_call_target="tpu_custom_call" | custom-call | tf_op jit(solution)/shard_map/pallas_call | solution.py:416
  113.3 2.9 %shard_map.77 = (bf16[128,2,1024]{2,1,0:T(2,128)(2,1)}, bf16[2,1024,512]{2,1,0:T(8,128)(2,1)}, bf16[2,512,1024]{2,1,0:T(8,128)(2,1)}) custom-call(bf16[2,1024,128]{2,1,0:T(8,128)(2,1)S(1)} %bitcast.1, bf16[128,2,1024]{2,1,0:T(2,128)(2,1)S(1)} %copy-done, bf16[2,1024,512]{2,1,0:T(8,128)(2,1)S(1)} %get-tuple-element.7.grad_in, ...), custom_call_target="tpu_custom_call" | custom-call | tf_op jit(solution)/shard_map/pallas_call | solution.py:456
Async XLA Ops:
  0.6 1.0 copy-start
  1.7 1.0 copy-start.1
  2.7 0.7 copy-start.2
